TPU v7x, 32 devices: a whole 2x2x4 slice. The times are simulated.
32 devices in a mesh: bin: 8 (over y, x, core), dp: 4 (over z).
Axes of the slice: x: 2, y: 2, z: 4, core: 2. Of those that a mesh axis runs over, the one named last changes fastest.
Arguments:
- peak_bins: int32 [512, 128], P('dp'), may hold values from 0 to 196607
- peak_values: bfloat16 [512, 128], P('dp'), may hold values from 0.049804688 to 1
- enc_weight: bfloat16 [196608, 2048], P(('bin', 'dp')), may hold values from -0.5 to 0.5
- enc_bias: float32 [2048], replicated, may hold values from -3 to 3
- dec_weight: bfloat16 [2048, 196608], P(None, ('bin', 'dp')), may hold values from -0.0007324219 to 0.0007324219
Outputs:
- grad_enc: bfloat16 [196608, 2048], P(('bin', 'dp'))
- grad_dec: bfloat16 [2048, 196608], P(None, ('bin', 'dp'))
All inputs are finite; a program needn't handle non-finite values.
Results may differ from a plain program's by a relative error of at most 0.0057.
Values may be sent and summed in bfloat16 or wider, within the bound.
A program may use at most 192 MiB of HBM per device.

v0:
```python
import jax
import jax.numpy as jnp
from jax import lax
from jax.sharding import PartitionSpec as P


def activation(values):
    return jax.nn.gelu(values, approximate=True)


def slope_times(pre, back):
    _, pullback = jax.vjp(activation, pre)
    return pullback(back)[0].astype(jnp.bfloat16)


def on_device(peak_bins, peak_values, enc_weight, enc_bias, dec_weight):
    bins_dev = enc_weight.shape[0]
    first_bin = (lax.axis_index("bin") * lax.axis_size("dp") + lax.axis_index("dp")) * bins_dev
    all_bins = lax.all_gather(peak_bins, "dp", axis=0, tiled=True)
    all_values = lax.all_gather(peak_values, "dp", axis=0, tiled=True)
    total_rows = all_bins.shape[0]
    local_bins = all_bins - first_bin
    inside = (local_bins >= 0) & (local_bins < bins_dev)
    row_ids = jnp.broadcast_to(jnp.arange(total_rows, dtype=jnp.int32)[:, None], all_bins.shape)
    dense = (
        jnp.zeros((total_rows, bins_dev), jnp.float32)
        .at[row_ids, jnp.where(inside, local_bins, 0)]
        .add(jnp.where(inside, all_values.astype(jnp.float32), 0.0))
        .astype(jnp.bfloat16)
    )
    partial_pre = jnp.dot(dense, enc_weight, preferred_element_type=jnp.float32)
    own_pre = (
        lax.psum(lax.psum_scatter(partial_pre, "dp", scatter_dimension=0, tiled=True), "bin")
        + enc_bias
    )
    hidden = lax.all_gather(activation(own_pre).astype(jnp.bfloat16), "dp", axis=0, tiled=True)
    recon = jnp.dot(hidden, dec_weight, preferred_element_type=jnp.float32)
    resid = (recon - dense.astype(jnp.float32)).astype(jnp.bfloat16)
    grad_dec = lax.dot_general(
        hidden, resid, (((0,), (0,)), ((), ())), preferred_element_type=jnp.float32
    ).astype(jnp.bfloat16)
    partial_back = lax.dot_general(
        resid, dec_weight, (((1,), (1,)), ((), ())), preferred_element_type=jnp.float32
    )
    own_back = lax.psum(
        lax.psum_scatter(partial_back, "dp", scatter_dimension=0, tiled=True), "bin"
    )
    dpre = lax.all_gather(slope_times(own_pre, own_back), "dp", axis=0, tiled=True)
    grad_enc = lax.dot_general(
        dense, dpre, (((0,), (0,)), ((), ())), preferred_element_type=jnp.float32
    ).astype(jnp.bfloat16)
    return (grad_enc, grad_dec)


def solution(mesh):
    placed = (P("dp", None), P("dp", None), P(("bin", "dp"), None), P(), P(None, ("bin", "dp")))
    return jax.shard_map(
        on_device,
        mesh=mesh,
        in_specs=placed,
        out_specs=(P(("bin", "dp"), None), P(None, ("bin", "dp"))),
        check_vma=False,
    )
```

profile of v0, /device:TPU:0, one launch (start us, length us, event | category | flops | bytes accessed | tf_op | source)
XLA Modules:
  0.0 963.0 jit_solution(2082393893302078359)
XLA Ops:
  7.2 0.0 reduce-scatter.3.cloned.1.call-start
  7.2 15.3 %all_gather.13 = bf16[512,128]{1,0:T(8,128)(2,1)S(1)} all-gather(bf16[128,128]{1,0:T(8,128)(2,1)} %param.6), channel_id=1, replica_groups=mesh['bin'=8,'dp'=4] {'dp'}, dimensions={0}, use_global_device_ids=true | all-gather | bytes 163840 | tf_op jit(solution)/shard_map/all_gather | solution.py:20
  22.5 14.5 %all_gather.12 = s32[512,128]{1,0:T(8,128)S(1)} all-gather(s32[128,128]{1,0:T(8,128)} %param.5), channel_id=1, replica_groups=mesh['bin'=8,'dp'=4] {'dp'}, dimensions={0}, use_global_device_ids=true | all-gather | bytes 327680 | tf_op jit(solution)/shard_map/all_gather | solution.py:19
  37.0 0.1 fusion.10
  37.1 0.1 select_bitcast_fusion.1
  37.2 0.8 and_reduce_fusion
  38.0 0.8 multiply_reduce_fusion
  38.8 444.7 %scatter_custom_fusion = f32[3145728]{0:T(1024)} fusion(s32[65536]{0:T(1024)S(1)} %select_bitcast_fusion, f32[65536]{0:T(1024)S(1)} %select_bitcast_fusion.1, f32[]{:T(128)} %constant.13.clone.1), kind=kCustom, calls=%fused_computation.5 | custom fusion | flops 65536 | bytes 12582916
  483.5 7.9 convert_element_type.32
  491.4 10.0 %reshape.21 = bf16[512,6144]{1,0:T(8,128)(2,1)} reshape(bf16[3145728]{0:T(1024)(128)(2,1)} %convert_element_type.32) | data formatting | bytes 12582912 | tf_op jit(solution)/shard_map/convert_element_type | solution.py:29
  501.5 0.0 copy-start.1
  501.5 21.0 %fusion.11 = f32[512,2048]{1,0:T(8,128)} fusion(bf16[512,6144]{1,0:T(8,128)(2,1)} %reshape.21, bf16[6144,2048]{1,0:T(8,128)(2,1)} %param.7), kind=kOutput, calls=%fused_computation.25 | convolution fusion | flops 12884901888 | bytes 35651584 | tf_op jit(solution)/shard_map/dot_general | solution.py:31
  522.5 0.0 reduce-scatter.3.cloned.1.call-update
  522.5 0.0 all-reduce.3.cloned.1.call-start
  522.5 78.0 %reduce-scatter.3.cloned.1.call-done = f32[128,2048]{1,0:T(8,128)} async-done(((f32[512,2048]{1,0:T(8,128)}), f32[128,2048]{1,0:T(8,128)}) %reduce-scatter.3.cloned.1.call-update) | async-done | bytes 1048592 | tf_op jit(solution)/shard_map/reduce_scatter | solution.py:33
  600.5 0.0 all-reduce.3.cloned.1.call-update
  600.5 0.0 all-gather.3.cloned.1.call-start
  600.6 60.5 %all-reduce.3.cloned.1.call-done = f32[128,2048]{1,0:T(8,128)} async-done(((f32[128,2048]{1,0:T(8,128)}), f32[128,2048]{1,0:T(8,128)}) %all-reduce.3.cloned.1.call-update) | async-done | bytes 1048592 | tf_op jit(solution)/shard_map/psum | solution.py:33
  661.1 0.0 copy-done.1
  661.1 2.4 multiply_convert_fusion
  663.5 0.0 all-gather.3.cloned.1.call-update
  663.5 0.2 reduce-scatter.5.cloned.1.call-start
  663.7 44.9 %all-gather.3.cloned.1.call-done = bf16[512,2048]{1,0:T(8,128)(2,1)} async-done(((bf16[128,2048]{1,0:T(8,128)(2,1)}), bf16[512,2048]{1,0:T(8,128)(2,1)}) %all-gather.3.cloned.1.call-update) | async-done | bytes 2097168 | tf_op jit(solution)/shard_map/all_gather | solution.py:36
  708.7 21.2 %fusion.12 = f32[512,6144]{1,0:T(8,128)} fusion(bf16[512,2048]{1,0:T(8,128)(2,1)} %all-gather.3.cloned.1.call-done, bf16[2048,6144]{1,0:T(8,128)(2,1)} %param.9), kind=kOutput, calls=%fused_computation.26 | convolution fusion | flops 12884901888 | bytes 39845888 | tf_op jit(solution)/shard_map/dot_general | solution.py:37
  729.9 0.0 copy-start
  729.9 0.0 copy-start.2
  729.9 21.7 %fusion = f32[512,2048]{1,0:T(8,128)} fusion(bf16[2048,6144]{1,0:T(8,128)(2,1)} %param.9, f32[512,6144]{1,0:T(8,128)} %fusion.12, bf16[512,6144]{1,0:T(8,128)(2,1)} %reshape.21), kind=kOutput, calls=%fused_computation.4 | convolution fusion | flops 12894339072 | bytes 48234496 | tf_op jit(solution)/shard_map/dot_general | solution.py:42
  751.6 0.0 reduce-scatter.5.cloned.1.call-update
  751.6 0.0 all-reduce.5.cloned.1.call-start
  751.6 75.6 %reduce-scatter.5.cloned.1.call-done = f32[128,2048]{1,0:T(8,128)} async-done(((f32[512,2048]{1,0:T(8,128)}), f32[128,2048]{1,0:T(8,128)}) %reduce-scatter.5.cloned.1.call-update) | async-done | bytes 1048592 | tf_op jit(solution)/shard_map/reduce_scatter | solution.py:46
  827.2 0.0 all-reduce.5.cloned.1.call-update
  827.3 0.3 all-gather.5.cloned.1.call-start
  827.5 59.8 %all-reduce.5.cloned.1.call-done = f32[128,2048]{1,0:T(8,128)} async-done(((f32[128,2048]{1,0:T(8,128)}), f32[128,2048]{1,0:T(8,128)}) %all-reduce.5.cloned.1.call-update) | async-done | bytes 1048592 | tf_op jit(solution)/shard_map/psum | solution.py:45
  887.4 0.0 copy-done
  887.4 2.8 fusion.9
  890.2 0.0 all-gather.5.cloned.1.call-update
  890.2 0.0 copy-done.2
  890.2 23.4 %convolution_convert_fusion.1 = bf16[2048,6144]{1,0:T(8,128)(2,1)} fusion(bf16[512,2048]{1,0:T(8,128)(2,1)S(1)} %copy-done.2, f32[512,6144]{1,0:T(8,128)} %fusion.12, bf16[512,6144]{1,0:T(8,128)(2,1)} %reshape.21), kind=kOutput, calls=%fused_computation.2 | convolution fusion | flops 12906921984 | bytes 46137344 | tf_op jit(solution)/shard_map/dot_general | solution.py:39
  913.6 21.7 %all-gather.5.cloned.1.call-done = bf16[512,2048]{1,0:T(8,128)(2,1)} async-done(((bf16[128,2048]{1,0:T(8,128)(2,1)}), bf16[512,2048]{1,0:T(8,128)(2,1)}) %all-gather.5.cloned.1.call-update) | async-done | bytes 2097168 | tf_op jit(solution)/shard_map/all_gather | solution.py:48
  935.3 20.9 %convolution_convert_fusion = bf16[6144,2048]{1,0:T(8,128)(2,1)} fusion(bf16[512,6144]{1,0:T(8,128)(2,1)} %reshape.21, bf16[512,2048]{1,0:T(8,128)(2,1)} %all-gather.5.cloned.1.call-done), kind=kOutput, calls=%fused_computation.1 | convolution fusion | flops 12897484800 | bytes 33554432 | tf_op jit(solution)/shard_map/dot_general | solution.py:49
  (2 shorter events, 0.1 us)
Async XLA Ops:
  7.2 593.3 %reduce-scatter.3.cloned.1.call-start = ((), (), s32[]{:S(2)}) async-start(), calls=%async_computation.2 | async-start | bytes 5242880 | tf_op jit(solution)/shard_map/reduce_scatter | solution.py:33
  501.5 159.7 %copy-start.1 = (f32[2048]{0:T(1024)S(1)}, f32[2048]{0:T(1024)}, u32[]{:S(2)}) copy-start(f32[2048]{0:T(1024)} %param.8) | copy-start | bytes 24580
  522.5 138.6 %all-reduce.3.cloned.1.call-start = ((), (), s32[]{:S(2)}) async-start(), calls=%async_computation.3 | async-start | bytes 2097152 | tf_op jit(solution)/shard_map/psum | solution.py:33
  600.5 108.1 %all-gather.3.cloned.1.call-start = ((), (), s32[]{:S(2)}) async-start(), calls=%async_computation.4 | async-start | bytes 2621440 | tf_op jit(solution)/shard_map/all_gather | solution.py:36
  663.5 163.7 %reduce-scatter.5.cloned.1.call-start = ((), (), s32[]{:S(2)}) async-start(), calls=%async_computation.5 | async-start | bytes 5242880 | tf_op jit(solution)/shard_map/reduce_scatter | solution.py:46
  729.9 157.5 %copy-start = (f32[128,2048]{1,0:T(8,128)S(1)}, f32[128,2048]{1,0:T(8,128)}, u32[]{:S(2)}) copy-start(f32[128,2048]{1,0:T(8,128)} %all-reduce.3.cloned.1.call-done) | copy-start | bytes 3145732
  729.9 160.3 %copy-start.2 = (bf16[512,2048]{1,0:T(8,128)(2,1)S(1)}, bf16[512,2048]{1,0:T(8,128)(2,1)}, u32[]{:S(2)}) copy-start(bf16[512,2048]{1,0:T(8,128)(2,1)} %all-gather.3.cloned.1.call-done) | copy-start | bytes 6291460
  751.6 135.8 %all-reduce.5.cloned.1.call-start = ((), (), s32[]{:S(2)}) async-start(), calls=%async_computation.6 | async-start | bytes 2097152 | tf_op jit(solution)/shard_map/psum | solution.py:45
  827.3 108.1 %all-gather.5.cloned.1.call-start = ((), (), s32[]{:S(2)}) async-start(), calls=%async_computation.7 | async-start | bytes 2621440 | tf_op jit(solution)/shard_map/all_gather | solution.py:48
Sparse Core Ops, SparseCore 0:
  522.6 77.8 reduce-scatter.2
  604.0 57.0 all-reduce.2
  663.6 44.9 all-gather.2
  751.7 75.4 reduce-scatter.4
  830.2 57.0 all-reduce.4
  890.3 44.9 all-gather.4
where the time goes:
time: 964 us; the launch traced here: 963 us
  other arithmetic  460 us (48%)
  waiting for transfers between devices  341 us (35%)
  matrix products  108 us (11%)
  blocking collectives  29.8 us (3%)
  between operations  14.2 us (1%)
  local copies, waits for them, and re-layouts  10.1 us (1%)
    unnamed x4, other arithmetic  446 us
    reduce_scatter x1, waiting for transfers between devices, on_device(): lax.psum_scatter(partial_pre, 'dp', scatter_dimension=0, tiled=True)  78 us
    reduce_scatter x1, waiting for transfers between devices, on_device(): lax.psum_scatter(partial_back, 'dp', scatter_dimension=0, tiled=True)  75.6 us
    psum x1, waiting for transfers between devices, on_device(): lax.psum(lax.psum_scatter(partial_pre, 'dp', scatter_dimension=0, tiled=T...  60.5 us
    psum x1, waiting for transfers between devices, on_device(): lax.psum(lax.psum_scatter(partial_back, 'dp', scatter_dimension=0, tiled=...  59.8 us
    all_gather x1, waiting for transfers between devices, on_device(): lax.all_gather(activation(own_pre).astype(jnp.bfloat16), 'dp', axis=0, ti...  44.9 us
    dot_general x1, matrix products, on_device(): lax.dot_general(hidden, resid, (((0,), (0,)), ((), ())), preferred_elemen...  23.4 us
    all_gather x1, waiting for transfers between devices, on_device(): lax.all_gather(slope_times(own_pre, own_back), 'dp', axis=0, tiled=True)  21.7 us
  transfers between devices with their start and end apart: 6, of which 6 were waited for; matrix products, arithmetic and copies ran while one was open for 2% of the time, Pallas kernels for 0%

commit v1 on v0

v1 whole, which is shorter than its diff:
```python
import functools

import jax
import jax.numpy as jnp
from jax import lax
from jax.experimental import pallas as pl
from jax.experimental.pallas import tpu as pltpu
from jax.sharding import PartitionSpec as P

AXES = ("bin", "dp")
LOW = 256
GROUP = 8


def activation(values):
    return jax.nn.gelu(values, approximate=True)


def slope_times(pre, back):
    _, pullback = jax.vjp(activation, pre)
    return pullback(back)[0].astype(jnp.bfloat16)


def spread_kernel(highs, bins_ref, values_ref, dense_ref):
    rows = GROUP * highs
    row_ids = lax.broadcasted_iota(jnp.int32, (rows, 128), 0)
    low_ids = lax.broadcasted_iota(jnp.int32, (LOW, 128), 0)
    sums = []
    for half in range(2):
        total = jnp.zeros((rows, LOW), jnp.float32)
        picks, lows = [], []
        for s in range(GROUP):
            row = half * GROUP + s
            local = bins_ref[row : row + 1, :]
            value = values_ref[row : row + 1, :]
            high = jnp.where(local < 0, -1, lax.shift_right_arithmetic(local, 8))
            key = jnp.where(high < 0, -1, high * GROUP + s)
            low = lax.bitwise_and(local, LOW - 1)
            picks.append(jnp.where(row_ids == key, value, 0.0).astype(jnp.bfloat16))
            lows.append(jnp.where(low_ids == low, 1.0, 0.0).astype(jnp.bfloat16))
        sums.append(
            lax.dot_general(
                jnp.concatenate(picks, axis=1),
                jnp.concatenate(lows, axis=1),
                (((1,), (1,)), ((), ())),
                preferred_element_type=jnp.float32,
            )
        )
    for high in range(highs):
        part = slice(high * GROUP, (high + 1) * GROUP)
        dense_ref[:, high * LOW : (high + 1) * LOW] = jnp.concatenate(
            [sums[0][part], sums[1][part]], axis=0
        ).astype(jnp.bfloat16)


def spread(local_bins, values, bins_dev):
    rows, peaks = local_bins.shape
    return pl.pallas_call(
        functools.partial(spread_kernel, bins_dev // LOW),
        grid=(rows // (2 * GROUP),),
        out_shape=jax.ShapeDtypeStruct((rows, bins_dev), jnp.bfloat16),
        in_specs=[pl.BlockSpec((2 * GROUP, peaks), lambda i: (i, 0))] * 2,
        out_specs=pl.BlockSpec((2 * GROUP, bins_dev), lambda i: (i, 0)),
        compiler_params=pltpu.CompilerParams(vmem_limit_bytes=32 * 2**20),
    )(local_bins, values)


def on_device(peak_bins, peak_values, enc_weight, enc_bias, dec_weight):
    bins_dev = enc_weight.shape[0]
    first_bin = (lax.axis_index("bin") * lax.axis_size("dp") + lax.axis_index("dp")) * bins_dev
    both = jnp.stack([peak_bins.astype(jnp.float32), peak_values.astype(jnp.float32)])
    both = lax.all_gather(both, "dp", axis=1, tiled=True)
    dense = spread(both[0].astype(jnp.int32) - first_bin, both[1], bins_dev)
    partial_pre = jnp.dot(dense, enc_weight, preferred_element_type=jnp.float32)
    own_pre = lax.psum_scatter(partial_pre, AXES, scatter_dimension=0, tiled=True) + enc_bias
    hidden = lax.all_gather(activation(own_pre).astype(jnp.bfloat16), AXES, axis=0, tiled=True)
    recon = jnp.dot(hidden, dec_weight, preferred_element_type=jnp.float32)
    resid = (recon - dense.astype(jnp.float32)).astype(jnp.bfloat16)
    partial_back = lax.dot_general(
        resid, dec_weight, (((1,), (1,)), ((), ())), preferred_element_type=jnp.float32
    )
    own_back = lax.psum_scatter(partial_back, AXES, scatter_dimension=0, tiled=True)
    grad_dec = lax.dot_general(
        hidden, resid, (((0,), (0,)), ((), ())), preferred_element_type=jnp.float32
    ).astype(jnp.bfloat16)
    dpre = lax.all_gather(slope_times(own_pre, own_back), AXES, axis=0, tiled=True)
    grad_enc = lax.dot_general(
        dense, dpre, (((0,), (0,)), ((), ())), preferred_element_type=jnp.float32
    ).astype(jnp.bfloat16)
    return (grad_enc, grad_dec)


def solution(mesh):
    placed = (P("dp", None), P("dp", None), P(AXES, None), P(), P(None, AXES))
    return jax.shard_map(
        on_device,
        mesh=mesh,
        in_specs=placed,
        out_specs=(P(AXES, None), P(None, AXES)),
        check_vma=False,
    )
```

time: 964 us -> 550 us (0.57)
  other arithmetic: 460 us -> 4.86 us
  waiting for transfers between devices: 341 us -> 387 us
  Pallas kernels: 0 us -> 17.3 us
  blocking collectives: 29.8 us -> 17.4 us
    unnamed x4 -> x0, other arithmetic: 446 us -> none
    reduce_scatter x2, waiting for transfers between devices: 154 us -> 296 us  [the longest x1 150 us: on_device(): lax.psum_scatter(partial_pre, AXES, scatter_dimension=0, tiled=True)]
    psum x2 -> x0, waiting for transfers between devices: 120 us -> none  [the longest x1 60.5 us: on_device(): lax.psum(lax.psum_scatter(partial_pre, 'dp', scatter_dimension=0, tiled=T...]
    all_gather x2, waiting for transfers between devices: 66.7 us -> 90.2 us  [the longest x1 57 us: on_device(): lax.all_gather(activation(own_pre).astype(jnp.bfloat16), AXES, axis=0, ti...]
    pallas_call x0 -> x1, Pallas kernels: none -> 17.3 us  [spread(): pl.pallas_call(functools.partial(spread_kernel, bins_dev // LOW), grid=(r...]
    all_gather x2 -> x1, blocking collectives: 29.8 us -> 17.4 us  [on_device(): both = lax.all_gather(both, 'dp', axis=1, tiled=True)]
    convert_element_type x1 -> x0, local copies, waits for them, and re-layouts: 10 us -> none  [on_device(): dense = jnp.zeros((total_rows, bins_dev), jnp.float32).at[row_ids, jnp.wh...]
  transfers between devices with their start and end apart: 6 -> 4, of which waited for: 6 -> 4; matrix products, arithmetic and copies ran while one was open for 2% -> 4% of each run, Pallas kernels for 0% -> 0%
where the time goes in v1:
time: 550 us
  waiting for transfers between devices  387 us (70%)
  matrix products  106 us (19%)
  blocking collectives  17.4 us (3%)
  Pallas kernels  17.3 us (3%)
  between operations  13.8 us (3%)
    reduce_scatter x1, waiting for transfers between devices, on_device(): lax.psum_scatter(partial_pre, AXES, scatter_dimension=0, tiled=True)  150 us
    reduce_scatter x1, waiting for transfers between devices, on_device(): lax.psum_scatter(partial_back, AXES, scatter_dimension=0, tiled=True)  147 us
    all_gather x1, waiting for transfers between devices, on_device(): lax.all_gather(activation(own_pre).astype(jnp.bfloat16), AXES, axis=0, ti...  57 us
    all_gather x1, waiting for transfers between devices, on_device(): lax.all_gather(slope_times(own_pre, own_back), AXES, axis=0, tiled=True)  33.2 us
    dot_general x1, matrix products, on_device(): lax.dot_general(hidden, resid, (((0,), (0,)), ((), ())), preferred_elemen...  23.2 us
    dot_general x1, matrix products, on_device(): lax.dot_general(resid, dec_weight, (((1,), (1,)), ((), ())), preferred_el...  21.7 us
    dot_general x1, matrix products, on_device(): recon = jnp.dot(hidden, dec_weight, preferred_element_type=jnp.float32)  21.2 us
    dot_general x1, matrix products, on_device(): lax.dot_general(dense, dpre, (((0,), (0,)), ((), ())), preferred_element_...  20.9 us
  transfers between devices with their start and end apart: 4, of which 4 were waited for; matrix products, arithmetic and copies ran while one was open for 4% of the time, Pallas kernels for 0%

profile of v1, /device:TPU:0, one launch (start us, length us, event | category | flops | bytes accessed | tf_op | source)
XLA Modules:
  0.0 549.8 jit_solution(2308492066666910602)
XLA Ops:
  7.2 0.0 reduce-scatter.3.cloned.1.call-start
  7.2 0.8 convert_bitcast_fusion
  8.1 0.8 bitcast_convert_fusion
  8.8 17.4 %all_gather.9 = f32[2,512,128]{2,1,0:T(8,128)S(1)} all-gather(f32[2,128,128]{2,1,0:T(8,128)S(1)} %pad_maximum_fusion), channel_id=1, replica_groups=mesh['bin'=8,'dp'=4] {'dp'}, dimensions={1}, use_global_device_ids=true | all-gather | bytes 655360 | tf_op jit(solution)/shard_map/all_gather | solution.py:72
  26.3 17.3 %shard_map.68 = bf16[512,6144]{1,0:T(8,128)(2,1)S(1)} custom-call(s32[512,128]{1,0:T(8,128)S(1)} %fusion.2.bins_ref, f32[512,128]{1,0:T(8,128)S(1)} %slice_bitcast_fusion.values_ref), custom_call_target="tpu_custom_call" | custom-call | tf_op jit(solution)/shard_map/pallas_call | solution.py:58
  43.5 0.0 copy-start
  43.5 2.7 copy-done
  46.2 0.0 copy-start.2
  46.2 19.4 %fusion.10 = f32[512,2048]{1,0:T(8,128)} fusion(bf16[512,6144]{1,0:T(8,128)(2,1)S(1)} %shard_map.68, bf16[6144,2048]{1,0:T(8,128)(2,1)} %param.7), kind=kOutput, calls=%fused_computation.21 | convolution fusion | flops 12884901888 | bytes 35651584 | tf_op jit(solution)/shard_map/dot_general | solution.py:74
  65.6 0.0 reduce-scatter.3.cloned.1.call-update
  65.7 0.0 all-gather.3.cloned.1.call-start
  65.7 150.0 %reduce-scatter.3.cloned.1.call-done = f32[16,2048]{1,0:T(8,128)} async-done(((f32[512,2048]{1,0:T(8,128)}), f32[16,2048]{1,0:T(8,128)}) %reduce-scatter.3.cloned.1.call-update) | async-done | bytes 131088 | tf_op jit(solution)/shard_map/reduce_scatter | solution.py:75
  215.7 0.0 copy-done.2
  215.7 1.6 multiply_convert_fusion
  217.3 0.0 all-gather.3.cloned.1.call-update
  217.3 0.2 reduce-scatter.5.cloned.1.call-start
  217.5 57.0 %all-gather.3.cloned.1.call-done = bf16[512,2048]{1,0:T(8,128)(2,1)} async-done(((bf16[16,2048]{1,0:T(8,128)(2,1)}), bf16[512,2048]{1,0:T(8,128)(2,1)}) %all-gather.3.cloned.1.call-update) | async-done | bytes 2097168 | tf_op jit(solution)/shard_map/all_gather | solution.py:76
  274.5 21.2 %fusion.11 = f32[512,6144]{1,0:T(8,128)} fusion(bf16[512,2048]{1,0:T(8,128)(2,1)} %all-gather.3.cloned.1.call-done, bf16[2048,6144]{1,0:T(8,128)(2,1)} %param.9), kind=kOutput, calls=%fused_computation.22 | convolution fusion | flops 12884901888 | bytes 39845888 | tf_op jit(solution)/shard_map/dot_general | solution.py:77
  295.7 0.0 copy-start.1
  295.7 0.0 copy-start.3
  295.7 21.7 %fusion = f32[512,2048]{1,0:T(8,128)} fusion(bf16[2048,6144]{1,0:T(8,128)(2,1)} %param.9, f32[512,6144]{1,0:T(8,128)} %fusion.11, bf16[512,6144]{1,0:T(8,128)(2,1)} %copy-done), kind=kOutput, calls=%fused_computation.3 | convolution fusion | flops 12894339072 | bytes 48234496 | tf_op jit(solution)/shard_map/dot_general | solution.py:79
  317.4 0.0 reduce-scatter.5.cloned.1.call-update
  317.4 0.3 all-gather.5.cloned.1.call-start
  317.7 146.5 %reduce-scatter.5.cloned.1.call-done = f32[16,2048]{1,0:T(8,128)} async-done(((f32[512,2048]{1,0:T(8,128)}), f32[16,2048]{1,0:T(8,128)}) %reduce-scatter.5.cloned.1.call-update) | async-done | bytes 131088 | tf_op jit(solution)/shard_map/reduce_scatter | solution.py:82
  464.3 0.0 copy-done.1
  464.3 1.6 fusion.9
  465.9 0.0 all-gather.5.cloned.1.call-update
  465.9 0.0 copy-done.3
  465.9 23.2 %convolution_convert_fusion.1 = bf16[2048,6144]{1,0:T(8,128)(2,1)} fusion(bf16[512,2048]{1,0:T(8,128)(2,1)S(1)} %copy-done.3, f32[512,6144]{1,0:T(8,128)} %fusion.11, bf16[512,6144]{1,0:T(8,128)(2,1)} %copy-done), kind=kOutput, calls=%fused_computation.1 | convolution fusion | flops 12906921984 | bytes 46137344 | tf_op jit(solution)/shard_map/dot_general | solution.py:83
  489.2 33.2 %all-gather.5.cloned.1.call-done = bf16[512,2048]{1,0:T(8,128)(2,1)} async-done(((bf16[16,2048]{1,0:T(8,128)(2,1)}), bf16[512,2048]{1,0:T(8,128)(2,1)}) %all-gather.5.cloned.1.call-update) | async-done | bytes 2097168 | tf_op jit(solution)/shard_map/all_gather | solution.py:86
  522.4 20.9 %convolution_convert_fusion = bf16[6144,2048]{1,0:T(8,128)(2,1)} fusion(bf16[512,6144]{1,0:T(8,128)(2,1)} %copy-done, bf16[512,2048]{1,0:T(8,128)(2,1)} %all-gather.5.cloned.1.call-done), kind=kOutput, calls=%fused_computation | convolution fusion | flops 12897484800 | bytes 33554432 | tf_op jit(solution)/shard_map/dot_general | solution.py:87
  (3 shorter events, 0.1 us)
Async XLA Ops:
  7.2 208.5 %reduce-scatter.3.cloned.1.call-start = ((), (), s32[]{:S(2)}) async-start(), calls=%async_computation.2 | async-start | bytes 4325376 | tf_op jit(solution)/shard_map/reduce_scatter | solution.py:75
  43.5 2.7 copy-start
  46.2 169.5 %copy-start.2 = (f32[2048]{0:T(1024)S(1)}, f32[2048]{0:T(1024)}, u32[]{:S(2)}) copy-start(f32[2048]{0:T(1024)} %param.8) | copy-start | bytes 24580
  65.7 208.9 %all-gather.3.cloned.1.call-start = ((), (), s32[]{:S(2)}) async-start(), calls=%async_computation.3 | async-start | bytes 2162688 | tf_op jit(solution)/shard_map/all_gather | solution.py:76
  217.3 247.0 %reduce-scatter.5.cloned.1.call-start = ((), (), s32[]{:S(2)}) async-start(), calls=%async_computation.4 | async-start | bytes 4325376 | tf_op jit(solution)/shard_map/reduce_scatter | solution.py:82
  295.7 168.5 %copy-start.1 = (f32[16,2048]{1,0:T(8,128)S(1)}, f32[16,2048]{1,0:T(8,128)}, u32[]{:S(2)}) copy-start(f32[16,2048]{1,0:T(8,128)} %reduce-scatter.3.cloned.1.call-done) | copy-start | bytes 393220
  295.7 170.2 %copy-start.3 = (bf16[512,2048]{1,0:T(8,128)(2,1)S(1)}, bf16[512,2048]{1,0:T(8,128)(2,1)}, u32[]{:S(2)}) copy-start(bf16[512,2048]{1,0:T(8,128)(2,1)} %all-gather.3.cloned.1.call-done) | copy-start | bytes 6291460
  317.4 204.9 %all-gather.5.cloned.1.call-start = ((), (), s32[]{:S(2)}) async-start(), calls=%async_computation.5 | async-start | bytes 2162688 | tf_op jit(solution)/shard_map/all_gather | solution.py:86
Sparse Core Ops, SparseCore 0:
  65.8 149.8 reduce-scatter.2
  219.2 55.3 all-gather.2
  317.6 146.6 reduce-scatter.4
  467.0 55.2 all-gather.4

commit v2 on v1

--- a/solution.py
+++ b/solution.py
@@ -65,25 +65,79 @@
     )(local_bins, values)
 
 
+def stages(part):
+    bits = {name: lax.axis_size(name).bit_length() - 1 for name in AXES}
+    others = list(range(1, bits["bin"]))
+    if part:
+        others = others[::-1]
+    return (
+        [("bin", bit) for bit in [0] + others] + [("dp", bit) for bit in range(bits["dp"])]
+    )
+
+
+def swap(values, name, bit):
+    pairs = [(i, i ^ (1 << bit)) for i in range(lax.axis_size(name))]
+    return lax.ppermute(values, name, pairs)
+
+
+def bit_of(name, bit):
+    return lax.bitwise_and(lax.shift_right_logical(lax.axis_index(name), bit), 1)
+
+
+def scatter_sum(values, part, narrow):
+    for name, bit in stages(part):
+        half = values.shape[0] // 2
+        mine = bit_of(name, bit)
+        keep = lax.dynamic_slice_in_dim(values, mine * half, half, 0)
+        send = lax.dynamic_slice_in_dim(values, (1 - mine) * half, half, 0)
+        if narrow and name == "bin" and bit > 0:
+            send = send.astype(jnp.bfloat16)
+        values = keep + swap(send, name, bit).astype(jnp.float32)
+    return values
+
+
+def gather(values, part):
+    for name, bit in stages(part)[::-1]:
+        theirs = swap(values, name, bit)
+        values = jnp.where(
+            bit_of(name, bit) == 0,
+            jnp.concatenate([values, theirs], axis=0),
+            jnp.concatenate([theirs, values], axis=0),
+        )
+    return values
+
+
 def on_device(peak_bins, peak_values, enc_weight, enc_bias, dec_weight):
     bins_dev = enc_weight.shape[0]
     first_bin = (lax.axis_index("bin") * lax.axis_size("dp") + lax.axis_index("dp")) * bins_dev
     both = jnp.stack([peak_bins.astype(jnp.float32), peak_values.astype(jnp.float32)])
     both = lax.all_gather(both, "dp", axis=1, tiled=True)
     dense = spread(both[0].astype(jnp.int32) - first_bin, both[1], bins_dev)
-    partial_pre = jnp.dot(dense, enc_weight, preferred_element_type=jnp.float32)
-    own_pre = lax.psum_scatter(partial_pre, AXES, scatter_dimension=0, tiled=True) + enc_bias
-    hidden = lax.all_gather(activation(own_pre).astype(jnp.bfloat16), AXES, axis=0, tiled=True)
-    recon = jnp.dot(hidden, dec_weight, preferred_element_type=jnp.float32)
-    resid = (recon - dense.astype(jnp.float32)).astype(jnp.bfloat16)
-    partial_back = lax.dot_general(
-        resid, dec_weight, (((1,), (1,)), ((), ())), preferred_element_type=jnp.float32
-    )
-    own_back = lax.psum_scatter(partial_back, AXES, scatter_dimension=0, tiled=True)
+    rows = dense.shape[0] // 2
+    parts = (0, 1)
+    dense_of = [dense[part * rows : (part + 1) * rows] for part in parts]
+    partial_pre = [
+        jnp.dot(dense_of[part], enc_weight, preferred_element_type=jnp.float32) for part in parts
+    ]
+    own_pre = [scatter_sum(partial_pre[part], part, False) + enc_bias for part in parts]
+    hidden_of = [gather(activation(own_pre[part]).astype(jnp.bfloat16), part) for part in parts]
+    resid_of, own_back = [], []
+    for part in parts:
+        recon = jnp.dot(hidden_of[part], dec_weight, preferred_element_type=jnp.float32)
+        resid = (recon - dense_of[part].astype(jnp.float32)).astype(jnp.bfloat16)
+        partial_back = lax.dot_general(
+            resid, dec_weight, (((1,), (1,)), ((), ())), preferred_element_type=jnp.float32
+        )
+        resid_of.append(resid)
+        own_back.append(scatter_sum(partial_back, part, True))
+    hidden = jnp.concatenate(hidden_of, axis=0)
+    resid = jnp.concatenate(resid_of, axis=0)
     grad_dec = lax.dot_general(
         hidden, resid, (((0,), (0,)), ((), ())), preferred_element_type=jnp.float32
     ).astype(jnp.bfloat16)
-    dpre = lax.all_gather(slope_times(own_pre, own_back), AXES, axis=0, tiled=True)
+    dpre = jnp.concatenate(
+        [gather(slope_times(own_pre[part], own_back[part]), part) for part in parts], axis=0
+    )
     grad_enc = lax.dot_general(
         dense, dpre, (((0,), (0,)), ((), ())), preferred_element_type=jnp.float32
     ).astype(jnp.bfloat16)

time: 550 us -> 291 us (0.53)
  waiting for transfers between devices: 387 us -> 64.2 us
  starting transfers between devices: 0.56 us -> 53.9 us
  matrix products: 106 us -> 123 us
  between operations: 13.8 us -> 1.22 us
    reduce_scatter x2 -> x0, waiting for transfers between devices: 296 us -> none  [the longest x1 150 us: on_device(): lax.psum_scatter(partial_pre, AXES, scatter_dimension=0, tiled=True)]
    all_gather x2 -> x0, waiting for transfers between devices: 90.2 us -> none  [the longest x1 57 us: on_device(): lax.all_gather(activation(own_pre).astype(jnp.bfloat16), AXES, axis=0, ti...]
    ppermute x0 -> x40, waiting for transfers between devices: none -> 64.2 us  [swap(): return lax.ppermute(values, name, pairs)]
    ppermute x0 -> x40, starting transfers between devices: none -> 53.9 us  [swap(): return lax.ppermute(values, name, pairs)]
    dot_general x2 -> x4, matrix products: 40.6 us -> 59 us  [the longest x2 33.4 us: on_device(): jnp.dot(hidden_of[part], dec_weight, preferred_element_type=jnp.float32)]
    dot_general x1 -> x2, matrix products: 21.7 us -> 25 us  [on_device(): lax.dot_general(resid, dec_weight, (((1,), (1,)), ((), ())), preferred_el...]
  transfers between devices with their start and end apart: 4 -> 40, of which waited for: 4 -> 25; matrix products, arithmetic and copies ran while one was open for 4% -> 34% of each run, Pallas kernels for 0% -> 0%
where the time goes in v2:
time: 291 us; the launch traced here: 290 us
  matrix products  123 us (42%)
  waiting for transfers between devices  64.2 us (22%)
  starting transfers between devices  53.9 us (19%)
  blocking collectives  17.4 us (6%)
  Pallas kernels  17.3 us (6%)
  other arithmetic  8.8 us (3%)
  local copies, waits for them, and re-layouts  4.96 us (2%)
    ppermute x40, waiting for transfers between devices, swap(): return lax.ppermute(values, name, pairs)  64.2 us
    ppermute x40, starting transfers between devices, swap(): return lax.ppermute(values, name, pairs)  53.9 us
    dot_general x2, matrix products, on_device(): jnp.dot(hidden_of[part], dec_weight, preferred_element_type=jnp.float32)  33.4 us
    dot_general x2, matrix products, on_device(): jnp.dot(dense_of[part], enc_weight, preferred_element_type=jnp.float32)  25.6 us
    dot_general x2, matrix products, on_device(): lax.dot_general(resid, dec_weight, (((1,), (1,)), ((), ())), preferred_el...  25 us
    dot_general x1, matrix products, on_device(): lax.dot_general(dense, dpre, (((0,), (0,)), ((), ())), preferred_element_...  19.7 us
    dot_general x1, matrix products, on_device(): lax.dot_general(hidden, resid, (((0,), (0,)), ((), ())), preferred_elemen...  19.1 us
    all_gather x1, blocking collectives, on_device(): both = lax.all_gather(both, 'dp', axis=1, tiled=True)  17.4 us
  transfers between devices with their start and end apart: 40, of which 25 were waited for; matrix products, arithmetic and copies ran while one was open for 34% of the time, Pallas kernels for 0%

profile of v2, /device:TPU:0, one launch (start us, length us, event | category | flops | bytes accessed | tf_op | source)
XLA Modules:
  0.0 290.4 jit_solution(16541039819536837136)
XLA Ops:
  2.3 17.4 %all_gather.3 = f32[2,512,128]{2,1,0:T(8,128)S(1)} all-gather(f32[2,128,128]{2,1,0:T(8,128)S(1)} %pad_maximum_fusion), channel_id=1, replica_groups=mesh['bin'=8,'dp'=4] {'dp'}, dimensions={1}, use_global_device_ids=true | all-gather | bytes 655360 | tf_op jit(solution)/shard_map/all_gather | solution.py:114
  19.7 17.3 %shard_map.68 = bf16[512,6144]{1,0:T(8,128)(2,1)S(1)} custom-call(s32[512,128]{1,0:T(8,128)S(1)} %fusion.16.bins_ref, f32[512,128]{1,0:T(8,128)S(1)} %slice_bitcast_fusion.values_ref), custom_call_target="tpu_custom_call" | custom-call | tf_op jit(solution)/shard_map/pallas_call | solution.py:58
  37.0 13.9 %fusion.5 = f32[256,2048]{1,0:T(8,128)S(1)} fusion(bf16[6144,2048]{1,0:T(8,128)(2,1)} %param.7, bf16[512,6144]{1,0:T(8,128)(2,1)S(1)} %shard_map.68), kind=kOutput, calls=%fused_computation.9 | convolution fusion | flops 6442450944 | bytes 30408704 | tf_op jit(solution)/shard_map/dot_general | solution.py:120
  52.1 11.7 %fusion.7 = f32[256,2048]{1,0:T(8,128)S(1)} fusion(bf16[6144,2048]{1,0:T(8,128)(2,1)} %param.7, bf16[512,6144]{1,0:T(8,128)(2,1)S(1)} %shard_map.68), kind=kOutput, calls=%fused_computation.11 | convolution fusion | flops 6442450944 | bytes 30408704 | tf_op jit(solution)/shard_map/dot_general | solution.py:120
  64.4 1.7 dynamic-slice_add_fusion.1
  66.1 1.6 collective-permute-start.21
  69.1 1.6 collective-permute-start.1
  70.7 9.4 %collective-permute-done.21 = f32[64,2048]{1,0:T(8,128)S(1)} collective-permute-done((f32[64,2048]{1,0:T(8,128)S(1)}, f32[64,2048]{1,0:T(8,128)S(1)}, u32[]{:S(2)}, u32[]{:S(2)}) %collective-permute-start.21) | collective-permute-done | bytes 524320 | tf_op jit(solution)/shard_map/ppermute | solution.py:80
  80.2 1.6 collective-permute-start.22
  81.8 1.7 collective-permute-done.1
  84.6 3.8 %collective-permute-done.22 = f32[32,2048]{1,0:T(8,128)S(1)} collective-permute-done((f32[32,2048]{1,0:T(8,128)S(1)}, f32[32,2048]{1,0:T(8,128)S(1)}, u32[]{:S(2)}, u32[]{:S(2)}) %collective-permute-start.22) | collective-permute-done | bytes 262176 | tf_op jit(solution)/shard_map/ppermute | solution.py:80
  88.5 2.2 collective-permute-start.23
  90.8 1.8 collective-permute-start.3
  92.5 2.4 collective-permute-done.23
  95.0 2.7 collective-permute-start.24
  97.7 2.0 collective-permute-start.4
  99.7 1.7 collective-permute-done.24
  101.4 1.6 collective-permute-done.4
  103.0 2.0 collective-permute-start.25
  105.1 2.9 %collective-permute-done.25 = bf16[8,2048]{1,0:T(8,128)(2,1)S(1)} collective-permute-done((bf16[8,2048]{1,0:T(8,128)(2,1)S(1)}, bf16[8,2048]{1,0:T(8,128)(2,1)S(1)}, u32[]{:S(2)}, u32[]{:S(2)}) %collective-permute-start.25) | collective-permute-done | bytes 32800 | tf_op jit(solution)/shard_map/ppermute | solution.py:80
  108.0 1.7 collective-permute-start.26
  109.7 2.9 collective-permute-start.5
  115.7 2.1 collective-permute-done.27
  117.8 1.5 collective-permute-start.28
  120.5 3.8 %collective-permute-done.28 = bf16[64,2048]{1,0:T(8,128)(2,1)S(1)} collective-permute-done((bf16[64,2048]{1,0:T(8,128)(2,1)S(1)}, bf16[64,2048]{1,0:T(8,128)(2,1)S(1)}, u32[]{:S(2)}, u32[]{:S(2)}) %collective-permute-start.28) | collective-permute-done | bytes 262176 | tf_op jit(solution)/shard_map/ppermute | solution.py:80
  127.2 6.1 %collective-permute-done.8 = bf16[64,2048]{1,0:T(8,128)(2,1)S(1)} collective-permute-done((bf16[64,2048]{1,0:T(8,128)(2,1)S(1)}, bf16[64,2048]{1,0:T(8,128)(2,1)S(1)}, u32[]{:S(2)}, u32[]{:S(2)}) %collective-permute-start.8) | collective-permute-done | bytes 262176 | tf_op jit(solution)/shard_map/ppermute | solution.py:80
  134.7 16.7 %fusion.1 = bf16[256,6144]{1,0:T(8,128)(2,1)} fusion(bf16[256,2048]{1,0:T(8,128)(2,1)S(1)} %maximum_select_fusion.2, bf16[2048,6144]{1,0:T(8,128)(2,1)} %param.9, bf16[512,6144]{1,0:T(8,128)(2,1)} %copy-done), kind=kOutput, calls=%fused_computation.5 | convolution fusion | flops 6447169536 | bytes 32505856 | tf_op jit(solution)/shard_map/dot_general | solution.py:126
  151.4 12.5 %fusion.34 = f32[256,2048]{1,0:T(8,128)S(1)} fusion(bf16[256,6144]{1,0:T(8,128)(2,1)} %fusion.1, bf16[2048,6144]{1,0:T(8,128)(2,1)} %param.9), kind=kOutput, calls=%fused_computation.107 | convolution fusion | flops 6442450944 | bytes 30408704 | tf_op jit(solution)/shard_map/dot_general | solution.py:128
  166.9 16.7 %fusion = bf16[256,6144]{1,0:T(8,128)(2,1)} fusion(bf16[256,2048]{1,0:T(8,128)(2,1)S(1)} %maximum_select_fusion, bf16[2048,6144]{1,0:T(8,128)(2,1)} %param.9, bf16[512,6144]{1,0:T(8,128)(2,1)} %copy-done), kind=kOutput, calls=%fused_computation.4 | convolution fusion | flops 6447169536 | bytes 32505856 | tf_op jit(solution)/shard_map/dot_general | solution.py:126
  183.6 12.5 %fusion.33 = f32[256,2048]{1,0:T(8,128)S(1)} fusion(bf16[256,6144]{1,0:T(8,128)(2,1)} %fusion, bf16[2048,6144]{1,0:T(8,128)(2,1)} %param.9), kind=kOutput, calls=%fused_computation.106 | convolution fusion | flops 6442450944 | bytes 30408704 | tf_op jit(solution)/shard_map/dot_general | solution.py:128
  196.5 1.7 dynamic-slice_add_fusion
  198.2 1.5 collective-permute-start.31
  199.8 1.6 collective-permute-start.11
  201.4 5.4 %collective-permute-done.31 = bf16[64,2048]{1,0:T(8,128)(2,1)S(1)} collective-permute-done((bf16[64,2048]{1,0:T(8,128)(2,1)S(1)}, bf16[64,2048]{1,0:T(8,128)(2,1)S(1)}, u32[]{:S(2)}, u32[]{:S(2)}) %collective-permute-start.31) | collective-permute-done | bytes 262176 | tf_op jit(solution)/shard_map/ppermute | solution.py:80
  208.4 1.6 collective-permute-start.12
  210.0 1.9 collective-permute-done.32
  215.0 2.4 collective-permute-done.33
  217.4 3.7 %collective-permute-start.34 = (f32[8,2048]{1,0:T(8,128)S(1)}, f32[8,2048]{1,0:T(8,128)S(1)}, u32[]{:S(2)}, u32[]{:S(2)}) collective-permute-start(f32[8,2048]{1,0:T(8,128)S(1)} %constant_dynamic-slice_fusion), channel_id=1, source_target_pairs={{0,2},{1,3},{2,0},{3,1},{4,6},{5,7},{6,4},{7,5},{8,10},{9,11},{10,... | collective-permute-start | bytes 196616 | tf_op jit(solution)/shard_map/ppermute | solution.py:80
  221.2 1.8 collective-permute-start.14
  224.4 3.4 %collective-permute-done.14 = f32[8,2048]{1,0:T(8,128)S(1)} collective-permute-done((f32[8,2048]{1,0:T(8,128)S(1)}, f32[8,2048]{1,0:T(8,128)S(1)}, u32[]{:S(2)}, u32[]{:S(2)}) %collective-permute-start.14) | collective-permute-done | bytes 65568 | tf_op jit(solution)/shard_map/ppermute | solution.py:80
  228.4 2.5 collective-permute-start.35
  230.9 2.2 collective-permute-done.15
  233.7 2.8 collective-permute-start.36
  238.8 1.6 collective-permute-start.37
  240.4 3.0 %collective-permute-done.17 = bf16[32,2048]{1,0:T(8,128)(2,1)S(1)} collective-permute-done((bf16[32,2048]{1,0:T(8,128)(2,1)S(1)}, bf16[32,2048]{1,0:T(8,128)(2,1)S(1)}, u32[]{:S(2)}, u32[]{:S(2)}) %collective-permute-start.17) | collective-permute-done | bytes 131104 | tf_op jit(solution)/shard_map/ppermute | solution.py:80
  245.6 4.2 %collective-permute-done.18 = bf16[64,2048]{1,0:T(8,128)(2,1)S(1)} collective-permute-done((bf16[64,2048]{1,0:T(8,128)(2,1)S(1)}, bf16[64,2048]{1,0:T(8,128)(2,1)S(1)}, u32[]{:S(2)}, u32[]{:S(2)}) %collective-permute-start.18) | collective-permute-done | bytes 262176 | tf_op jit(solution)/shard_map/ppermute | solution.py:80
  251.1 19.1 %convolution_convert_fusion.1 = bf16[2048,6144]{1,0:T(8,128)(2,1)} fusion(bf16[256,6144]{1,0:T(8,128)(2,1)S(1)} %copy-done.8, bf16[256,6144]{1,0:T(8,128)(2,1)} %fusion, bf16[256,2048]{1,0:T(8,128)(2,1)S(1)} %copy-done.4, bf16[256,2048]{1,0:T(8,128)(2,1)S(1)} %copy-done.6), kind=kOutput, calls=%fused_computation.1 | convolution fusion | flops 12914262016 | bytes 33554432 | tf_op jit(solution)/shard_map/dot_general | solution.py:135
  270.7 19.7 %convolution_convert_fusion = bf16[6144,2048]{1,0:T(8,128)(2,1)} fusion(bf16[512,6144]{1,0:T(8,128)(2,1)} %copy-done, bf16[256,2048]{1,0:T(8,128)(2,1)S(1)} %maximum_select_fusion.3, bf16[256,2048]{1,0:T(8,128)(2,1)S(1)} %maximum_select_fusion.1), kind=kOutput, calls=%fused_computation | convolution fusion | flops 12901679104 | bytes 33554432 | tf_op jit(solution)/shard_map/dot_general | solution.py:141
  (123 shorter events, 31.9 us)
Async XLA Ops:
  37.0 15.1 %copy-start = (bf16[512,6144]{1,0:T(8,128)(2,1)}, bf16[512,6144]{1,0:T(8,128)(2,1)S(1)}, u32[]{:S(2)}) copy-start(bf16[512,6144]{1,0:T(8,128)(2,1)S(1)} %shard_map.68) | copy-start | bytes 18874372
  50.9 12.8 %copy-start.1 = (f32[256,2048]{1,0:T(8,128)}, f32[256,2048]{1,0:T(8,128)S(1)}, u32[]{:S(2)}) copy-start(f32[256,2048]{1,0:T(8,128)S(1)} %fusion.5) | copy-start | bytes 6291460
  52.1 12.4 %collective-permute-start.20 = (f32[128,2048]{1,0:T(8,128)}, f32[128,2048]{1,0:T(8,128)}, u32[]{:S(2)}, u32[]{:S(2)}) collective-permute-start(f32[128,2048]{1,0:T(8,128)} %constant_dynamic-slice_fusion.7), channel_id=1, source_target_pairs={{0,4},{4,0},{8,12},{12,8},{16,20},{20,16},{24,28},{28,24},{1,5},{5... | collective-permute-start | bytes 3145736 | tf_op jit(solution)/shard_map/ppermute | solution.py:80
  63.9 3.9 %collective-permute-start = (f32[128,2048]{1,0:T(8,128)S(1)}, f32[128,2048]{1,0:T(8,128)}, u32[]{:S(2)}, u32[]{:S(2)}) collective-permute-start(f32[128,2048]{1,0:T(8,128)S(1)} %constant_dynamic-slice_fusion.15), channel_id=1, source_target_pairs={{0,4},{4,0},{8,12},{12,8},{16,20},{20,16},{24,28},{28,24},{1,5},{5... | collective-permute-start | bytes 3145736 | tf_op jit(solution)/shard_map/ppermute | solution.py:80
  66.1 13.9 %collective-permute-start.21 = (f32[64,2048]{1,0:T(8,128)S(1)}, f32[64,2048]{1,0:T(8,128)S(1)}, u32[]{:S(2)}, u32[]{:S(2)}) collective-permute-start(f32[64,2048]{1,0:T(8,128)S(1)} %constant_dynamic-slice_fusion.6), channel_id=1, source_target_pairs={{0,16},{4,20},{8,24},{12,28},{16,0},{20,4},{24,8},{28,12},{1,17},{... | collective-permute-start | bytes 1572872 | tf_op jit(solution)/shard_map/ppermute | solution.py:80
  69.1 14.3 %collective-permute-start.1 = (f32[64,2048]{1,0:T(8,128)S(1)}, f32[64,2048]{1,0:T(8,128)S(1)}, u32[]{:S(2)}, u32[]{:S(2)}) collective-permute-start(f32[64,2048]{1,0:T(8,128)S(1)} %constant_dynamic-slice_fusion.14), channel_id=1, source_target_pairs={{0,8},{4,12},{8,0},{12,4},{16,24},{20,28},{24,16},{28,20},{1,9},{5... | collective-permute-start | bytes 1572872 | tf_op jit(solution)/shard_map/ppermute | solution.py:80
  80.2 22.8 %copy-start.7 = (f32[2048]{0:T(1024)S(1)}, f32[2048]{0:T(1024)}, u32[]{:S(2)}) copy-start(f32[2048]{0:T(1024)} %param.8) | copy-start | bytes 24580
  80.2 8.2 %collective-permute-start.22 = (f32[32,2048]{1,0:T(8,128)S(1)}, f32[32,2048]{1,0:T(8,128)S(1)}, u32[]{:S(2)}, u32[]{:S(2)}) collective-permute-start(f32[32,2048]{1,0:T(8,128)S(1)} %constant_dynamic-slice_fusion.5), channel_id=1, source_target_pairs={{0,8},{4,12},{8,0},{12,4},{16,24},{20,28},{24,16},{28,20},{1,9},{5... | collective-permute-start | bytes 786440 | tf_op jit(solution)/shard_map/ppermute | solution.py:80
  83.6 7.1 %collective-permute-start.2 = (f32[32,2048]{1,0:T(8,128)S(1)}, f32[32,2048]{1,0:T(8,128)S(1)}, u32[]{:S(2)}, u32[]{:S(2)}) collective-permute-start(f32[32,2048]{1,0:T(8,128)S(1)} %constant_dynamic-slice_fusion.13), channel_id=1, source_target_pairs={{0,16},{4,20},{8,24},{12,28},{16,0},{20,4},{24,8},{28,12},{1,17},{... | collective-permute-start | bytes 786440 | tf_op jit(solution)/shard_map/ppermute | solution.py:80
  88.5 6.5 %collective-permute-start.23 = (f32[16,2048]{1,0:T(8,128)S(1)}, f32[16,2048]{1,0:T(8,128)S(1)}, u32[]{:S(2)}, u32[]{:S(2)}) collective-permute-start(f32[16,2048]{1,0:T(8,128)S(1)} %constant_dynamic-slice_fusion.4), channel_id=1, source_target_pairs={{0,1},{1,0},{2,3},{3,2},{4,5},{5,4},{6,7},{7,6},{8,9},{9,8},{10,11... | collective-permute-start | bytes 393224 | tf_op jit(solution)/shard_map/ppermute | solution.py:80
  90.8 6.9 %collective-permute-start.3 = (f32[16,2048]{1,0:T(8,128)S(1)}, f32[16,2048]{1,0:T(8,128)S(1)}, u32[]{:S(2)}, u32[]{:S(2)}) collective-permute-start(f32[16,2048]{1,0:T(8,128)S(1)} %constant_dynamic-slice_fusion.12), channel_id=1, source_target_pairs={{0,1},{1,0},{2,3},{3,2},{4,5},{5,4},{6,7},{7,6},{8,9},{9,8},{10,11... | collective-permute-start | bytes 393224 | tf_op jit(solution)/shard_map/ppermute | solution.py:80
  95.0 6.4 %collective-permute-start.24 = (f32[8,2048]{1,0:T(8,128)S(1)}, f32[8,2048]{1,0:T(8,128)S(1)}, u32[]{:S(2)}, u32[]{:S(2)}) collective-permute-start(f32[8,2048]{1,0:T(8,128)S(1)} %constant_dynamic-slice_fusion.3), channel_id=1, source_target_pairs={{0,2},{1,3},{2,0},{3,1},{4,6},{5,7},{6,4},{7,5},{8,10},{9,11},{10,... | collective-permute-start | bytes 196616 | tf_op jit(solution)/shard_map/ppermute | solution.py:80
  97.7 5.2 %collective-permute-start.4 = (f32[8,2048]{1,0:T(8,128)S(1)}, f32[8,2048]{1,0:T(8,128)S(1)}, u32[]{:S(2)}, u32[]{:S(2)}) collective-permute-start(f32[8,2048]{1,0:T(8,128)S(1)} %constant_dynamic-slice_fusion.11), channel_id=1, source_target_pairs={{0,2},{1,3},{2,0},{3,1},{4,6},{5,7},{6,4},{7,5},{8,10},{9,11},{10,... | collective-permute-start | bytes 196616 | tf_op jit(solution)/shard_map/ppermute | solution.py:80
  103.0 5.0 %collective-permute-start.25 = (bf16[8,2048]{1,0:T(8,128)(2,1)S(1)}, bf16[8,2048]{1,0:T(8,128)(2,1)S(1)}, u32[]{:S(2)}, u32[]{:S(2)}) collective-permute-start(bf16[8,2048]{1,0:T(8,128)(2,1)S(1)} %get-tuple-element.5), channel_id=1, source_target_pairs={{0,2},{1,3},{2,0},{3,1},{4,6},{5,7},{6,4},{7,5},{8,10},{9,11},{10,... | collective-permute-start | bytes 98312 | tf_op jit(solution)/shard_map/ppermute | solution.py:80
  108.0 4.7 %collective-permute-start.26 = (bf16[16,2048]{1,0:T(8,128)(2,1)S(1)}, bf16[16,2048]{1,0:T(8,128)(2,1)S(1)}, u32[]{:S(2)}, u32[]{:S(2)}) collective-permute-start(bf16[16,2048]{1,0:T(8,128)(2,1)S(1)} %maximum_select_fusion.18), channel_id=1, source_target_pairs={{0,1},{1,0},{2,3},{3,2},{4,5},{5,4},{6,7},{7,6},{8,9},{9,8},{10,11... | collective-permute-start | bytes 196616 | tf_op jit(solution)/shard_map/ppermute | solution.py:80
  109.7 4.8 %collective-permute-start.5 = (bf16[8,2048]{1,0:T(8,128)(2,1)S(1)}, bf16[8,2048]{1,0:T(8,128)(2,1)S(1)}, u32[]{:S(2)}, u32[]{:S(2)}) collective-permute-start(bf16[8,2048]{1,0:T(8,128)(2,1)S(1)} %get-tuple-element.4), channel_id=1, source_target_pairs={{0,2},{1,3},{2,0},{3,1},{4,6},{5,7},{6,4},{7,5},{8,10},{9,11},{10,... | collective-permute-start | bytes 98312 | tf_op jit(solution)/shard_map/ppermute | solution.py:80
  112.7 5.0 %collective-permute-start.27 = (bf16[32,2048]{1,0:T(8,128)(2,1)S(1)}, bf16[32,2048]{1,0:T(8,128)(2,1)S(1)}, u32[]{:S(2)}, u32[]{:S(2)}) collective-permute-start(bf16[32,2048]{1,0:T(8,128)(2,1)S(1)} %maximum_select_fusion.14), channel_id=1, source_target_pairs={{0,8},{4,12},{8,0},{12,4},{16,24},{20,28},{24,16},{28,20},{1,9},{5... | collective-permute-start | bytes 393224 | tf_op jit(solution)/shard_map/ppermute | solution.py:80
  114.6 4.7 %collective-permute-start.6 = (bf16[16,2048]{1,0:T(8,128)(2,1)S(1)}, bf16[16,2048]{1,0:T(8,128)(2,1)S(1)}, u32[]{:S(2)}, u32[]{:S(2)}) collective-permute-start(bf16[16,2048]{1,0:T(8,128)(2,1)S(1)} %maximum_select_fusion.16), channel_id=1, source_target_pairs={{0,1},{1,0},{2,3},{3,2},{4,5},{5,4},{6,7},{7,6},{8,9},{9,8},{10,11... | collective-permute-start | bytes 196616 | tf_op jit(solution)/shard_map/ppermute | solution.py:80
  117.8 6.4 %collective-permute-start.28 = (bf16[64,2048]{1,0:T(8,128)(2,1)S(1)}, bf16[64,2048]{1,0:T(8,128)(2,1)S(1)}, u32[]{:S(2)}, u32[]{:S(2)}) collective-permute-start(bf16[64,2048]{1,0:T(8,128)(2,1)S(1)} %maximum_select_fusion.10), channel_id=1, source_target_pairs={{0,16},{4,20},{8,24},{12,28},{16,0},{20,4},{24,8},{28,12},{1,17},{... | collective-permute-start | bytes 786440 | tf_op jit(solution)/shard_map/ppermute | solution.py:80
  119.3 6.3 %collective-permute-start.7 = (bf16[32,2048]{1,0:T(8,128)(2,1)S(1)}, bf16[32,2048]{1,0:T(8,128)(2,1)S(1)}, u32[]{:S(2)}, u32[]{:S(2)}) collective-permute-start(bf16[32,2048]{1,0:T(8,128)(2,1)S(1)} %maximum_select_fusion.12), channel_id=1, source_target_pairs={{0,16},{4,20},{8,24},{12,28},{16,0},{20,4},{24,8},{28,12},{1,17},{... | collective-permute-start | bytes 393224 | tf_op jit(solution)/shard_map/ppermute | solution.py:80
  124.4 9.1 %collective-permute-start.29 = (bf16[128,2048]{1,0:T(8,128)(2,1)S(1)}, bf16[128,2048]{1,0:T(8,128)(2,1)S(1)}, u32[]{:S(2)}, u32[]{:S(2)}) collective-permute-start(bf16[128,2048]{1,0:T(8,128)(2,1)S(1)} %maximum_select_fusion.6), channel_id=1, source_target_pairs={{0,4},{4,0},{8,12},{12,8},{16,20},{20,16},{24,28},{28,24},{1,5},{5... | collective-permute-start | bytes 1572872 | tf_op jit(solution)/shard_map/ppermute | solution.py:80
  125.7 7.6 %collective-permute-start.8 = (bf16[64,2048]{1,0:T(8,128)(2,1)S(1)}, bf16[64,2048]{1,0:T(8,128)(2,1)S(1)}, u32[]{:S(2)}, u32[]{:S(2)}) collective-permute-start(bf16[64,2048]{1,0:T(8,128)(2,1)S(1)} %maximum_select_fusion.8), channel_id=1, source_target_pairs={{0,8},{4,12},{8,0},{12,4},{16,24},{20,28},{24,16},{28,20},{1,9},{5... | collective-permute-start | bytes 786440 | tf_op jit(solution)/shard_map/ppermute | solution.py:80
  133.4 32.2 %collective-permute-start.9 = (bf16[128,2048]{1,0:T(8,128)(2,1)S(1)}, bf16[128,2048]{1,0:T(8,128)(2,1)S(1)}, u32[]{:S(2)}, u32[]{:S(2)}) collective-permute-start(bf16[128,2048]{1,0:T(8,128)(2,1)S(1)} %maximum_select_fusion.4), channel_id=1, source_target_pairs={{0,4},{4,0},{8,12},{12,8},{16,20},{20,16},{24,28},{28,24},{1,5},{5... | collective-permute-start | bytes 1572872 | tf_op jit(solution)/shard_map/ppermute | solution.py:80
  163.9 2.0 copy-start.2
  165.1 31.3 %collective-permute-start.30 = (f32[128,2048]{1,0:T(8,128)}, f32[128,2048]{1,0:T(8,128)}, u32[]{:S(2)}, u32[]{:S(2)}) collective-permute-start(f32[128,2048]{1,0:T(8,128)} %constant_dynamic-slice_fusion.2), channel_id=1, source_target_pairs={{0,4},{4,0},{8,12},{12,8},{16,20},{20,16},{24,28},{28,24},{1,5},{5... | collective-permute-start | bytes 3145736 | tf_op jit(solution)/shard_map/ppermute | solution.py:80
  165.9 1.0 copy-start.5
  196.2 3.4 %collective-permute-start.10 = (f32[128,2048]{1,0:T(8,128)S(1)}, f32[128,2048]{1,0:T(8,128)S(1)}, u32[]{:S(2)}, u32[]{:S(2)}) collective-permute-start(f32[128,2048]{1,0:T(8,128)S(1)} %constant_dynamic-slice_fusion.10), channel_id=1, source_target_pairs={{0,4},{4,0},{8,12},{12,8},{16,20},{20,16},{24,28},{28,24},{1,5},{5... | collective-permute-start | bytes 3145736 | tf_op jit(solution)/shard_map/ppermute | solution.py:80
  198.2 8.6 %collective-permute-start.31 = (bf16[64,2048]{1,0:T(8,128)(2,1)S(1)}, bf16[64,2048]{1,0:T(8,128)(2,1)S(1)}, u32[]{:S(2)}, u32[]{:S(2)}) collective-permute-start(bf16[64,2048]{1,0:T(8,128)(2,1)S(1)} %dynamic-slice_convert_fusion), channel_id=1, source_target_pairs={{0,16},{4,20},{8,24},{12,28},{16,0},{20,4},{24,8},{28,12},{1,17},{... | collective-permute-start | bytes 786440 | tf_op jit(solution)/shard_map/ppermute | solution.py:80
  199.8 8.5 %collective-permute-start.11 = (bf16[64,2048]{1,0:T(8,128)(2,1)S(1)}, bf16[64,2048]{1,0:T(8,128)(2,1)S(1)}, u32[]{:S(2)}, u32[]{:S(2)}) collective-permute-start(bf16[64,2048]{1,0:T(8,128)(2,1)S(1)} %dynamic-slice_convert_fusion.1), channel_id=1, source_target_pairs={{0,8},{4,12},{8,0},{12,4},{16,24},{20,28},{24,16},{28,20},{1,9},{5... | collective-permute-start | bytes 786440 | tf_op jit(solution)/shard_map/ppermute | solution.py:80
  206.9 5.0 %collective-permute-start.32 = (bf16[32,2048]{1,0:T(8,128)(2,1)S(1)}, bf16[32,2048]{1,0:T(8,128)(2,1)S(1)}, u32[]{:S(2)}, u32[]{:S(2)}) collective-permute-start(bf16[32,2048]{1,0:T(8,128)(2,1)S(1)} %dynamic-slice_convert_fusion.2), channel_id=1, source_target_pairs={{0,8},{4,12},{8,0},{12,4},{16,24},{20,28},{24,16},{28,20},{1,9},{5... | collective-permute-start | bytes 393224 | tf_op jit(solution)/shard_map/ppermute | solution.py:80
  208.4 5.0 %collective-permute-start.12 = (bf16[32,2048]{1,0:T(8,128)(2,1)S(1)}, bf16[32,2048]{1,0:T(8,128)(2,1)S(1)}, u32[]{:S(2)}, u32[]{:S(2)}) collective-permute-start(bf16[32,2048]{1,0:T(8,128)(2,1)S(1)} %dynamic-slice_convert_fusion.3), channel_id=1, source_target_pairs={{0,16},{4,20},{8,24},{12,28},{16,0},{20,4},{24,8},{28,12},{1,17},{... | collective-permute-start | bytes 393224 | tf_op jit(solution)/shard_map/ppermute | solution.py:80
  212.0 39.1 %copy-start.4 = (bf16[256,2048]{1,0:T(8,128)(2,1)S(1)}, bf16[256,2048]{1,0:T(8,128)(2,1)}, u32[]{:S(2)}) copy-start(bf16[256,2048]{1,0:T(8,128)(2,1)} %copy-done.3) | copy-start | bytes 3145732
  212.0 39.1 %copy-start.6 = (bf16[256,2048]{1,0:T(8,128)(2,1)S(1)}, bf16[256,2048]{1,0:T(8,128)(2,1)}, u32[]{:S(2)}) copy-start(bf16[256,2048]{1,0:T(8,128)(2,1)} %copy-done.5) | copy-start | bytes 3145732
  212.0 39.1 %copy-start.8 = (bf16[256,6144]{1,0:T(8,128)(2,1)S(1)}, bf16[256,6144]{1,0:T(8,128)(2,1)}, u32[]{:S(2)}) copy-start(bf16[256,6144]{1,0:T(8,128)(2,1)} %fusion.1) | copy-start | bytes 9437188
  212.0 5.4 %collective-permute-start.33 = (f32[16,2048]{1,0:T(8,128)S(1)}, f32[16,2048]{1,0:T(8,128)S(1)}, u32[]{:S(2)}, u32[]{:S(2)}) collective-permute-start(f32[16,2048]{1,0:T(8,128)S(1)} %constant_dynamic-slice_fusion.1), channel_id=1, source_target_pairs={{0,1},{1,0},{2,3},{3,2},{4,5},{5,4},{6,7},{7,6},{8,9},{9,8},{10,11... | collective-permute-start | bytes 393224 | tf_op jit(solution)/shard_map/ppermute | solution.py:80
  213.5 7.6 %collective-permute-start.13 = (f32[16,2048]{1,0:T(8,128)S(1)}, f32[16,2048]{1,0:T(8,128)S(1)}, u32[]{:S(2)}, u32[]{:S(2)}) collective-permute-start(f32[16,2048]{1,0:T(8,128)S(1)} %constant_dynamic-slice_fusion.9), channel_id=1, source_target_pairs={{0,1},{1,0},{2,3},{3,2},{4,5},{5,4},{6,7},{7,6},{8,9},{9,8},{10,11... | collective-permute-start | bytes 393224 | tf_op jit(solution)/shard_map/ppermute | solution.py:80
  217.4 7.0 %collective-permute-start.34 = (f32[8,2048]{1,0:T(8,128)S(1)}, f32[8,2048]{1,0:T(8,128)S(1)}, u32[]{:S(2)}, u32[]{:S(2)}) collective-permute-start(f32[8,2048]{1,0:T(8,128)S(1)} %constant_dynamic-slice_fusion), channel_id=1, source_target_pairs={{0,2},{1,3},{2,0},{3,1},{4,6},{5,7},{6,4},{7,5},{8,10},{9,11},{10,... | collective-permute-start | bytes 196616 | tf_op jit(solution)/shard_map/ppermute | solution.py:80
  221.2 6.6 %collective-permute-start.14 = (f32[8,2048]{1,0:T(8,128)S(1)}, f32[8,2048]{1,0:T(8,128)S(1)}, u32[]{:S(2)}, u32[]{:S(2)}) collective-permute-start(f32[8,2048]{1,0:T(8,128)S(1)} %constant_dynamic-slice_fusion.8), channel_id=1, source_target_pairs={{0,2},{1,3},{2,0},{3,1},{4,6},{5,7},{6,4},{7,5},{8,10},{9,11},{10,... | collective-permute-start | bytes 196616 | tf_op jit(solution)/shard_map/ppermute | solution.py:80
  227.9 5.2 %collective-permute-start.15 = (bf16[8,2048]{1,0:T(8,128)(2,1)S(1)}, bf16[8,2048]{1,0:T(8,128)(2,1)S(1)}, u32[]{:S(2)}, u32[]{:S(2)}) collective-permute-start(bf16[8,2048]{1,0:T(8,128)(2,1)S(1)} %get-tuple-element.2), channel_id=1, source_target_pairs={{0,2},{1,3},{2,0},{3,1},{4,6},{5,7},{6,4},{7,5},{8,10},{9,11},{10,... | collective-permute-start | bytes 98312 | tf_op jit(solution)/shard_map/ppermute | solution.py:80
  228.4 5.3 %collective-permute-start.35 = (bf16[8,2048]{1,0:T(8,128)(2,1)S(1)}, bf16[8,2048]{1,0:T(8,128)(2,1)S(1)}, u32[]{:S(2)}, u32[]{:S(2)}) collective-permute-start(bf16[8,2048]{1,0:T(8,128)(2,1)S(1)} %get-tuple-element.3), channel_id=1, source_target_pairs={{0,2},{1,3},{2,0},{3,1},{4,6},{5,7},{6,4},{7,5},{8,10},{9,11},{10,... | collective-permute-start | bytes 98312 | tf_op jit(solution)/shard_map/ppermute | solution.py:80
  233.2 4.3 %collective-permute-start.16 = (bf16[16,2048]{1,0:T(8,128)(2,1)S(1)}, bf16[16,2048]{1,0:T(8,128)(2,1)S(1)}, u32[]{:S(2)}, u32[]{:S(2)}) collective-permute-start(bf16[16,2048]{1,0:T(8,128)(2,1)S(1)} %maximum_select_fusion.17), channel_id=1, source_target_pairs={{0,1},{1,0},{2,3},{3,2},{4,5},{5,4},{6,7},{7,6},{8,9},{9,8},{10,11... | collective-permute-start | bytes 196616 | tf_op jit(solution)/shard_map/ppermute | solution.py:80
  233.7 5.0 %collective-permute-start.36 = (bf16[16,2048]{1,0:T(8,128)(2,1)S(1)}, bf16[16,2048]{1,0:T(8,128)(2,1)S(1)}, u32[]{:S(2)}, u32[]{:S(2)}) collective-permute-start(bf16[16,2048]{1,0:T(8,128)(2,1)S(1)} %maximum_select_fusion.19), channel_id=1, source_target_pairs={{0,1},{1,0},{2,3},{3,2},{4,5},{5,4},{6,7},{7,6},{8,9},{9,8},{10,11... | collective-permute-start | bytes 196616 | tf_op jit(solution)/shard_map/ppermute | solution.py:80
  237.5 5.8 %collective-permute-start.17 = (bf16[32,2048]{1,0:T(8,128)(2,1)S(1)}, bf16[32,2048]{1,0:T(8,128)(2,1)S(1)}, u32[]{:S(2)}, u32[]{:S(2)}) collective-permute-start(bf16[32,2048]{1,0:T(8,128)(2,1)S(1)} %maximum_select_fusion.13), channel_id=1, source_target_pairs={{0,16},{4,20},{8,24},{12,28},{16,0},{20,4},{24,8},{28,12},{1,17},{... | collective-permute-start | bytes 393224 | tf_op jit(solution)/shard_map/ppermute | solution.py:80
  238.8 5.6 %collective-permute-start.37 = (bf16[32,2048]{1,0:T(8,128)(2,1)S(1)}, bf16[32,2048]{1,0:T(8,128)(2,1)S(1)}, u32[]{:S(2)}, u32[]{:S(2)}) collective-permute-start(bf16[32,2048]{1,0:T(8,128)(2,1)S(1)} %maximum_select_fusion.15), channel_id=1, source_target_pairs={{0,8},{4,12},{8,0},{12,4},{16,24},{20,28},{24,16},{28,20},{1,9},{5... | collective-permute-start | bytes 393224 | tf_op jit(solution)/shard_map/ppermute | solution.py:80
  243.4 6.4 %collective-permute-start.18 = (bf16[64,2048]{1,0:T(8,128)(2,1)S(1)}, bf16[64,2048]{1,0:T(8,128)(2,1)S(1)}, u32[]{:S(2)}, u32[]{:S(2)}) collective-permute-start(bf16[64,2048]{1,0:T(8,128)(2,1)S(1)} %maximum_select_fusion.9), channel_id=1, source_target_pairs={{0,8},{4,12},{8,0},{12,4},{16,24},{20,28},{24,16},{28,20},{1,9},{5... | collective-permute-start | bytes 786440 | tf_op jit(solution)/shard_map/ppermute | solution.py:80
  244.4 6.4 %collective-permute-start.38 = (bf16[64,2048]{1,0:T(8,128)(2,1)S(1)}, bf16[64,2048]{1,0:T(8,128)(2,1)S(1)}, u32[]{:S(2)}, u32[]{:S(2)}) collective-permute-start(bf16[64,2048]{1,0:T(8,128)(2,1)S(1)} %maximum_select_fusion.11), channel_id=1, source_target_pairs={{0,16},{4,20},{8,24},{12,28},{16,0},{20,4},{24,8},{28,12},{1,17},{... | collective-permute-start | bytes 786440 | tf_op jit(solution)/shard_map/ppermute | solution.py:80
  250.0 20.2 %collective-permute-start.19 = (bf16[128,2048]{1,0:T(8,128)(2,1)S(1)}, bf16[128,2048]{1,0:T(8,128)(2,1)S(1)}, u32[]{:S(2)}, u32[]{:S(2)}) collective-permute-start(bf16[128,2048]{1,0:T(8,128)(2,1)S(1)} %maximum_select_fusion.5), channel_id=1, source_target_pairs={{0,4},{4,0},{8,12},{12,8},{16,20},{20,16},{24,28},{28,24},{1,5},{5... | collective-permute-start | bytes 1572872 | tf_op jit(solution)/shard_map/ppermute | solution.py:80
  251.0 19.4 %collective-permute-start.39 = (bf16[128,2048]{1,0:T(8,128)(2,1)S(1)}, bf16[128,2048]{1,0:T(8,128)(2,1)S(1)}, u32[]{:S(2)}, u32[]{:S(2)}) collective-permute-start(bf16[128,2048]{1,0:T(8,128)(2,1)S(1)} %maximum_select_fusion.7), channel_id=1, source_target_pairs={{0,4},{4,0},{8,12},{12,8},{16,20},{20,16},{24,28},{28,24},{1,5},{5... | collective-permute-start | bytes 1572872 | tf_op jit(solution)/shard_map/ppermute | solution.py:80
  (1 other events, 1.0 us)

commit v3 on v2

--- a/solution.py
+++ b/solution.py
@@ -84,13 +84,13 @@
     return lax.bitwise_and(lax.shift_right_logical(lax.axis_index(name), bit), 1)
 
 
-def scatter_sum(values, part, narrow):
+def scatter_sum(values, part, narrow_axes):
     for name, bit in stages(part):
         half = values.shape[0] // 2
         mine = bit_of(name, bit)
         keep = lax.dynamic_slice_in_dim(values, mine * half, half, 0)
         send = lax.dynamic_slice_in_dim(values, (1 - mine) * half, half, 0)
-        if narrow and name == "bin" and bit > 0:
+        if name in narrow_axes and (name, bit) != ("bin", 0):
             send = send.astype(jnp.bfloat16)
         values = keep + swap(send, name, bit).astype(jnp.float32)
     return values
@@ -119,7 +119,7 @@
     partial_pre = [
         jnp.dot(dense_of[part], enc_weight, preferred_element_type=jnp.float32) for part in parts
     ]
-    own_pre = [scatter_sum(partial_pre[part], part, False) + enc_bias for part in parts]
+    own_pre = [scatter_sum(partial_pre[part], part, ("bin",)) + enc_bias for part in parts]
     hidden_of = [gather(activation(own_pre[part]).astype(jnp.bfloat16), part) for part in parts]
     resid_of, own_back = [], []
     for part in parts:
@@ -129,7 +129,7 @@
             resid, dec_weight, (((1,), (1,)), ((), ())), preferred_element_type=jnp.float32
         )
         resid_of.append(resid)
-        own_back.append(scatter_sum(partial_back, part, True))
+        own_back.append(scatter_sum(partial_back, part, AXES))
     hidden = jnp.concatenate(hidden_of, axis=0)
     resid = jnp.concatenate(resid_of, axis=0)
     grad_dec = lax.dot_general(

time: 291 us -> 280 us (0.962)
  waiting for transfers between devices: 64.2 us -> 51.6 us
    ppermute x40, waiting for transfers between devices: 64.2 us -> 51.6 us  [swap(): return lax.ppermute(values, name, pairs)]
  transfers between devices with their start and end apart: 40 -> 40, of which waited for: 25 -> 25; matrix products, arithmetic and copies ran while one was open for 34% -> 35% of each run, Pallas kernels for 0% -> 0%
where the time goes in v3:
time: 280 us
  matrix products  123 us (44%)
  starting transfers between devices  55.8 us (20%)
  waiting for transfers between devices  51.6 us (18%)
  blocking collectives  17.4 us (6%)
  Pallas kernels  17.3 us (6%)
  other arithmetic  8.77 us (3%)
  local copies, waits for them, and re-layouts  4.95 us (2%)
    ppermute x40, starting transfers between devices, swap(): return lax.ppermute(values, name, pairs)  55.8 us
    ppermute x40, waiting for transfers between devices, swap(): return lax.ppermute(values, name, pairs)  51.6 us
    dot_general x2, matrix products, on_device(): jnp.dot(hidden_of[part], dec_weight, preferred_element_type=jnp.float32)  33.4 us
    dot_general x2, matrix products, on_device(): jnp.dot(dense_of[part], enc_weight, preferred_element_type=jnp.float32)  25.6 us
    dot_general x2, matrix products, on_device(): lax.dot_general(resid, dec_weight, (((1,), (1,)), ((), ())), preferred_el...  25 us
    dot_general x1, matrix products, on_device(): lax.dot_general(dense, dpre, (((0,), (0,)), ((), ())), preferred_element_...  19.7 us
    dot_general x1, matrix products, on_device(): lax.dot_general(hidden, resid, (((0,), (0,)), ((), ())), preferred_elemen...  19.1 us
    all_gather x1, blocking collectives, on_device(): both = lax.all_gather(both, 'dp', axis=1, tiled=True)  17.4 us
  transfers between devices with their start and end apart: 40, of which 25 were waited for; matrix products, arithmetic and copies ran while one was open for 35% of the time, Pallas kernels for 0%

profile of v3, /device:TPU:0, one launch (start us, length us, event | category | flops | bytes accessed | tf_op | source)
XLA Modules:
  0.0 279.7 jit_solution(15586986991235364933)
XLA Ops:
  2.3 17.4 %all_gather.3 = f32[2,512,128]{2,1,0:T(8,128)S(1)} all-gather(f32[2,128,128]{2,1,0:T(8,128)S(1)} %pad_maximum_fusion), channel_id=1, replica_groups=mesh['bin'=8,'dp'=4] {'dp'}, dimensions={1}, use_global_device_ids=true | all-gather | bytes 655360 | tf_op jit(solution)/shard_map/all_gather | solution.py:114
  19.7 17.3 %shard_map.68 = bf16[512,6144]{1,0:T(8,128)(2,1)S(1)} custom-call(s32[512,128]{1,0:T(8,128)S(1)} %fusion.16.bins_ref, f32[512,128]{1,0:T(8,128)S(1)} %slice_bitcast_fusion.values_ref), custom_call_target="tpu_custom_call" | custom-call | tf_op jit(solution)/shard_map/pallas_call | solution.py:58
  37.0 13.9 %fusion.5 = f32[256,2048]{1,0:T(8,128)S(1)} fusion(bf16[6144,2048]{1,0:T(8,128)(2,1)} %param.7, bf16[512,6144]{1,0:T(8,128)(2,1)S(1)} %shard_map.68), kind=kOutput, calls=%fused_computation.9 | convolution fusion | flops 6442450944 | bytes 30408704 | tf_op jit(solution)/shard_map/dot_general | solution.py:120
  52.1 11.7 %fusion.7 = f32[256,2048]{1,0:T(8,128)S(1)} fusion(bf16[6144,2048]{1,0:T(8,128)(2,1)} %param.7, bf16[512,6144]{1,0:T(8,128)(2,1)S(1)} %shard_map.68), kind=kOutput, calls=%fused_computation.11 | convolution fusion | flops 6442450944 | bytes 30408704 | tf_op jit(solution)/shard_map/dot_general | solution.py:120
  64.4 1.7 dynamic-slice_add_fusion.1
  66.1 1.6 collective-permute-start.21
  69.1 1.6 collective-permute-start.1
  70.7 3.8 %collective-permute-done.21 = bf16[64,2048]{1,0:T(8,128)(2,1)S(1)} collective-permute-done((bf16[64,2048]{1,0:T(8,128)(2,1)S(1)}, bf16[64,2048]{1,0:T(8,128)(2,1)S(1)}, u32[]{:S(2)}, u32[]{:S(2)}) %collective-permute-start.21) | collective-permute-done | bytes 262176 | tf_op jit(solution)/shard_map/ppermute | solution.py:80
  74.6 1.6 collective-permute-start.22
  76.1 1.7 collective-permute-done.1
  80.0 2.2 collective-permute-start.23
  83.0 2.2 collective-permute-start.3
  86.6 2.7 collective-permute-start.24
  89.3 2.0 collective-permute-start.4
  91.3 1.7 collective-permute-done.24
  94.6 2.0 collective-permute-start.25
  96.6 3.0 %collective-permute-done.25 = bf16[8,2048]{1,0:T(8,128)(2,1)S(1)} collective-permute-done((bf16[8,2048]{1,0:T(8,128)(2,1)S(1)}, bf16[8,2048]{1,0:T(8,128)(2,1)S(1)}, u32[]{:S(2)}, u32[]{:S(2)}) %collective-permute-start.25) | collective-permute-done | bytes 32800 | tf_op jit(solution)/shard_map/ppermute | solution.py:80
  99.6 2.1 collective-permute-start.26
  101.7 2.7 collective-permute-start.5
  104.4 1.5 collective-permute-start.27
  107.6 1.9 collective-permute-done.27
  112.2 3.8 %collective-permute-done.28 = bf16[64,2048]{1,0:T(8,128)(2,1)S(1)} collective-permute-done((bf16[64,2048]{1,0:T(8,128)(2,1)S(1)}, bf16[64,2048]{1,0:T(8,128)(2,1)S(1)}, u32[]{:S(2)}, u32[]{:S(2)}) %collective-permute-start.28) | collective-permute-done | bytes 262176 | tf_op jit(solution)/shard_map/ppermute | solution.py:80
  117.4 1.5 collective-permute-start.8
  118.9 6.0 %collective-permute-done.8 = bf16[64,2048]{1,0:T(8,128)(2,1)S(1)} collective-permute-done((bf16[64,2048]{1,0:T(8,128)(2,1)S(1)}, bf16[64,2048]{1,0:T(8,128)(2,1)S(1)}, u32[]{:S(2)}, u32[]{:S(2)}) %collective-permute-start.8) | collective-permute-done | bytes 262176 | tf_op jit(solution)/shard_map/ppermute | solution.py:80
  126.4 16.7 %fusion.1 = bf16[256,6144]{1,0:T(8,128)(2,1)} fusion(bf16[256,2048]{1,0:T(8,128)(2,1)S(1)} %maximum_select_fusion.2, bf16[2048,6144]{1,0:T(8,128)(2,1)} %param.9, bf16[512,6144]{1,0:T(8,128)(2,1)} %copy-done), kind=kOutput, calls=%fused_computation.5 | convolution fusion | flops 6447169536 | bytes 32505856 | tf_op jit(solution)/shard_map/dot_general | solution.py:126
  143.0 12.5 %fusion.34 = f32[256,2048]{1,0:T(8,128)S(1)} fusion(bf16[256,6144]{1,0:T(8,128)(2,1)} %fusion.1, bf16[2048,6144]{1,0:T(8,128)(2,1)} %param.9), kind=kOutput, calls=%fused_computation.107 | convolution fusion | flops 6442450944 | bytes 30408704 | tf_op jit(solution)/shard_map/dot_general | solution.py:128
  158.6 16.7 %fusion = bf16[256,6144]{1,0:T(8,128)(2,1)} fusion(bf16[256,2048]{1,0:T(8,128)(2,1)S(1)} %maximum_select_fusion, bf16[2048,6144]{1,0:T(8,128)(2,1)} %param.9, bf16[512,6144]{1,0:T(8,128)(2,1)} %copy-done), kind=kOutput, calls=%fused_computation.4 | convolution fusion | flops 6447169536 | bytes 32505856 | tf_op jit(solution)/shard_map/dot_general | solution.py:126
  175.3 12.5 %fusion.33 = f32[256,2048]{1,0:T(8,128)S(1)} fusion(bf16[256,6144]{1,0:T(8,128)(2,1)} %fusion, bf16[2048,6144]{1,0:T(8,128)(2,1)} %param.9), kind=kOutput, calls=%fused_computation.106 | convolution fusion | flops 6442450944 | bytes 30408704 | tf_op jit(solution)/shard_map/dot_general | solution.py:128
  188.1 1.7 dynamic-slice_add_fusion
  191.1 1.6 collective-permute-start.11
  192.6 5.9 %collective-permute-done.31 = bf16[64,2048]{1,0:T(8,128)(2,1)S(1)} collective-permute-done((bf16[64,2048]{1,0:T(8,128)(2,1)S(1)}, bf16[64,2048]{1,0:T(8,128)(2,1)S(1)}, u32[]{:S(2)}, u32[]{:S(2)}) %collective-permute-start.31) | collective-permute-done | bytes 262176 | tf_op jit(solution)/shard_map/ppermute | solution.py:80
  198.6 1.5 collective-permute-start.32
  201.2 2.4 collective-permute-done.32
  203.7 1.6 collective-permute-start.33
  205.4 1.5 collective-permute-start.13
  208.1 2.8 collective-permute-start.34
  210.9 1.7 collective-permute-start.14
  212.9 3.0 %collective-permute-done.14 = bf16[8,2048]{1,0:T(8,128)(2,1)S(1)} collective-permute-done((bf16[8,2048]{1,0:T(8,128)(2,1)S(1)}, bf16[8,2048]{1,0:T(8,128)(2,1)S(1)}, u32[]{:S(2)}, u32[]{:S(2)}) %collective-permute-start.14) | collective-permute-done | bytes 32800 | tf_op jit(solution)/shard_map/ppermute | solution.py:80
  216.1 1.6 collective-permute-start.15
  219.1 2.0 collective-permute-done.15
  222.5 2.8 %collective-permute-start.36 = (bf16[16,2048]{1,0:T(8,128)(2,1)S(1)}, bf16[16,2048]{1,0:T(8,128)(2,1)S(1)}, u32[]{:S(2)}, u32[]{:S(2)}) collective-permute-start(bf16[16,2048]{1,0:T(8,128)(2,1)S(1)} %maximum_select_fusion.19), channel_id=1, source_target_pairs={{0,1},{1,0},{2,3},{3,2},{4,5},{5,4},{6,7},{7,6},{8,9},{9,8},{10,11... | collective-permute-start | bytes 196616 | tf_op jit(solution)/shard_map/ppermute | solution.py:80
  225.4 1.7 collective-permute-start.17
  229.0 2.9 %collective-permute-done.17 = bf16[32,2048]{1,0:T(8,128)(2,1)S(1)} collective-permute-done((bf16[32,2048]{1,0:T(8,128)(2,1)S(1)}, bf16[32,2048]{1,0:T(8,128)(2,1)S(1)}, u32[]{:S(2)}, u32[]{:S(2)}) %collective-permute-start.17) | collective-permute-done | bytes 131104 | tf_op jit(solution)/shard_map/ppermute | solution.py:80
  231.9 1.8 collective-permute-start.18
  235.0 3.3 %collective-permute-done.18 = bf16[64,2048]{1,0:T(8,128)(2,1)S(1)} collective-permute-done((bf16[64,2048]{1,0:T(8,128)(2,1)S(1)}, bf16[64,2048]{1,0:T(8,128)(2,1)S(1)}, u32[]{:S(2)}, u32[]{:S(2)}) %collective-permute-start.18) | collective-permute-done | bytes 262176 | tf_op jit(solution)/shard_map/ppermute | solution.py:80
  238.5 1.6 collective-permute-done.38
  240.4 19.1 %convolution_convert_fusion.1 = bf16[2048,6144]{1,0:T(8,128)(2,1)} fusion(bf16[256,6144]{1,0:T(8,128)(2,1)S(1)} %copy-done.8, bf16[256,6144]{1,0:T(8,128)(2,1)} %fusion, bf16[256,2048]{1,0:T(8,128)(2,1)S(1)} %copy-done.4, bf16[256,2048]{1,0:T(8,128)(2,1)S(1)} %copy-done.6), kind=kOutput, calls=%fused_computation.1 | convolution fusion | flops 12914262016 | bytes 33554432 | tf_op jit(solution)/shard_map/dot_general | solution.py:135
  260.0 19.7 %convolution_convert_fusion = bf16[6144,2048]{1,0:T(8,128)(2,1)} fusion(bf16[512,6144]{1,0:T(8,128)(2,1)} %copy-done, bf16[256,2048]{1,0:T(8,128)(2,1)S(1)} %maximum_select_fusion.3, bf16[256,2048]{1,0:T(8,128)(2,1)S(1)} %maximum_select_fusion.1), kind=kOutput, calls=%fused_computation | convolution fusion | flops 12901679104 | bytes 33554432 | tf_op jit(solution)/shard_map/dot_general | solution.py:141
  (123 shorter events, 32.5 us)
Async XLA Ops:
  37.0 15.1 %copy-start = (bf16[512,6144]{1,0:T(8,128)(2,1)}, bf16[512,6144]{1,0:T(8,128)(2,1)S(1)}, u32[]{:S(2)}) copy-start(bf16[512,6144]{1,0:T(8,128)(2,1)S(1)} %shard_map.68) | copy-start | bytes 18874372
  50.9 12.8 %copy-start.1 = (f32[256,2048]{1,0:T(8,128)}, f32[256,2048]{1,0:T(8,128)S(1)}, u32[]{:S(2)}) copy-start(f32[256,2048]{1,0:T(8,128)S(1)} %fusion.5) | copy-start | bytes 6291460
  52.1 12.4 %collective-permute-start.20 = (f32[128,2048]{1,0:T(8,128)}, f32[128,2048]{1,0:T(8,128)}, u32[]{:S(2)}, u32[]{:S(2)}) collective-permute-start(f32[128,2048]{1,0:T(8,128)} %constant_dynamic-slice_fusion.3), channel_id=1, source_target_pairs={{0,4},{4,0},{8,12},{12,8},{16,20},{20,16},{24,28},{28,24},{1,5},{5... | collective-permute-start | bytes 3145736 | tf_op jit(solution)/shard_map/ppermute | solution.py:80
  63.9 3.9 %collective-permute-start = (f32[128,2048]{1,0:T(8,128)S(1)}, f32[128,2048]{1,0:T(8,128)}, u32[]{:S(2)}, u32[]{:S(2)}) collective-permute-start(f32[128,2048]{1,0:T(8,128)S(1)} %constant_dynamic-slice_fusion.7), channel_id=1, source_target_pairs={{0,4},{4,0},{8,12},{12,8},{16,20},{20,16},{24,28},{28,24},{1,5},{5... | collective-permute-start | bytes 3145736 | tf_op jit(solution)/shard_map/ppermute | solution.py:80
  66.1 8.3 %collective-permute-start.21 = (bf16[64,2048]{1,0:T(8,128)(2,1)S(1)}, bf16[64,2048]{1,0:T(8,128)(2,1)S(1)}, u32[]{:S(2)}, u32[]{:S(2)}) collective-permute-start(bf16[64,2048]{1,0:T(8,128)(2,1)S(1)} %dynamic-slice_convert_fusion.1), channel_id=1, source_target_pairs={{0,16},{4,20},{8,24},{12,28},{16,0},{20,4},{24,8},{28,12},{1,17},{... | collective-permute-start | bytes 786440 | tf_op jit(solution)/shard_map/ppermute | solution.py:80
  69.1 25.4 %copy-start.7 = (f32[2048]{0:T(1024)S(1)}, f32[2048]{0:T(1024)}, u32[]{:S(2)}) copy-start(f32[2048]{0:T(1024)} %param.8) | copy-start | bytes 24580
  69.1 8.7 %collective-permute-start.1 = (bf16[64,2048]{1,0:T(8,128)(2,1)S(1)}, bf16[64,2048]{1,0:T(8,128)(2,1)S(1)}, u32[]{:S(2)}, u32[]{:S(2)}) collective-permute-start(bf16[64,2048]{1,0:T(8,128)(2,1)S(1)} %dynamic-slice_convert_fusion.3), channel_id=1, source_target_pairs={{0,8},{4,12},{8,0},{12,4},{16,24},{20,28},{24,16},{28,20},{1,9},{5... | collective-permute-start | bytes 786440 | tf_op jit(solution)/shard_map/ppermute | solution.py:80
  74.6 5.4 %collective-permute-start.22 = (bf16[32,2048]{1,0:T(8,128)(2,1)S(1)}, bf16[32,2048]{1,0:T(8,128)(2,1)S(1)}, u32[]{:S(2)}, u32[]{:S(2)}) collective-permute-start(bf16[32,2048]{1,0:T(8,128)(2,1)S(1)} %dynamic-slice_convert_fusion.5), channel_id=1, source_target_pairs={{0,8},{4,12},{8,0},{12,4},{16,24},{20,28},{24,16},{28,20},{1,9},{5... | collective-permute-start | bytes 393224 | tf_op jit(solution)/shard_map/ppermute | solution.py:80
  78.0 5.0 %collective-permute-start.2 = (bf16[32,2048]{1,0:T(8,128)(2,1)S(1)}, bf16[32,2048]{1,0:T(8,128)(2,1)S(1)}, u32[]{:S(2)}, u32[]{:S(2)}) collective-permute-start(bf16[32,2048]{1,0:T(8,128)(2,1)S(1)} %dynamic-slice_convert_fusion.7), channel_id=1, source_target_pairs={{0,16},{4,20},{8,24},{12,28},{16,0},{20,4},{24,8},{28,12},{1,17},{... | collective-permute-start | bytes 393224 | tf_op jit(solution)/shard_map/ppermute | solution.py:80
  80.0 6.5 %collective-permute-start.23 = (f32[16,2048]{1,0:T(8,128)S(1)}, f32[16,2048]{1,0:T(8,128)S(1)}, u32[]{:S(2)}, u32[]{:S(2)}) collective-permute-start(f32[16,2048]{1,0:T(8,128)S(1)} %constant_dynamic-slice_fusion.2), channel_id=1, source_target_pairs={{0,1},{1,0},{2,3},{3,2},{4,5},{5,4},{6,7},{7,6},{8,9},{9,8},{10,11... | collective-permute-start | bytes 393224 | tf_op jit(solution)/shard_map/ppermute | solution.py:80
  83.0 6.2 %collective-permute-start.3 = (f32[16,2048]{1,0:T(8,128)S(1)}, f32[16,2048]{1,0:T(8,128)S(1)}, u32[]{:S(2)}, u32[]{:S(2)}) collective-permute-start(f32[16,2048]{1,0:T(8,128)S(1)} %constant_dynamic-slice_fusion.6), channel_id=1, source_target_pairs={{0,1},{1,0},{2,3},{3,2},{4,5},{5,4},{6,7},{7,6},{8,9},{9,8},{10,11... | collective-permute-start | bytes 393224 | tf_op jit(solution)/shard_map/ppermute | solution.py:80
  86.6 6.4 %collective-permute-start.24 = (f32[8,2048]{1,0:T(8,128)S(1)}, f32[8,2048]{1,0:T(8,128)S(1)}, u32[]{:S(2)}, u32[]{:S(2)}) collective-permute-start(f32[8,2048]{1,0:T(8,128)S(1)} %constant_dynamic-slice_fusion.1), channel_id=1, source_target_pairs={{0,2},{1,3},{2,0},{3,1},{4,6},{5,7},{6,4},{7,5},{8,10},{9,11},{10,... | collective-permute-start | bytes 196616 | tf_op jit(solution)/shard_map/ppermute | solution.py:80
  89.3 5.2 %collective-permute-start.4 = (f32[8,2048]{1,0:T(8,128)S(1)}, f32[8,2048]{1,0:T(8,128)S(1)}, u32[]{:S(2)}, u32[]{:S(2)}) collective-permute-start(f32[8,2048]{1,0:T(8,128)S(1)} %constant_dynamic-slice_fusion.5), channel_id=1, source_target_pairs={{0,2},{1,3},{2,0},{3,1},{4,6},{5,7},{6,4},{7,5},{8,10},{9,11},{10,... | collective-permute-start | bytes 196616 | tf_op jit(solution)/shard_map/ppermute | solution.py:80
  94.6 5.0 %collective-permute-start.25 = (bf16[8,2048]{1,0:T(8,128)(2,1)S(1)}, bf16[8,2048]{1,0:T(8,128)(2,1)S(1)}, u32[]{:S(2)}, u32[]{:S(2)}) collective-permute-start(bf16[8,2048]{1,0:T(8,128)(2,1)S(1)} %get-tuple-element.5), channel_id=1, source_target_pairs={{0,2},{1,3},{2,0},{3,1},{4,6},{5,7},{6,4},{7,5},{8,10},{9,11},{10,... | collective-permute-start | bytes 98312 | tf_op jit(solution)/shard_map/ppermute | solution.py:80
  99.6 4.8 %collective-permute-start.26 = (bf16[16,2048]{1,0:T(8,128)(2,1)S(1)}, bf16[16,2048]{1,0:T(8,128)(2,1)S(1)}, u32[]{:S(2)}, u32[]{:S(2)}) collective-permute-start(bf16[16,2048]{1,0:T(8,128)(2,1)S(1)} %maximum_select_fusion.18), channel_id=1, source_target_pairs={{0,1},{1,0},{2,3},{3,2},{4,5},{5,4},{6,7},{7,6},{8,9},{9,8},{10,11... | collective-permute-start | bytes 196616 | tf_op jit(solution)/shard_map/ppermute | solution.py:80
  101.7 4.8 %collective-permute-start.5 = (bf16[8,2048]{1,0:T(8,128)(2,1)S(1)}, bf16[8,2048]{1,0:T(8,128)(2,1)S(1)}, u32[]{:S(2)}, u32[]{:S(2)}) collective-permute-start(bf16[8,2048]{1,0:T(8,128)(2,1)S(1)} %get-tuple-element.4), channel_id=1, source_target_pairs={{0,2},{1,3},{2,0},{3,1},{4,6},{5,7},{6,4},{7,5},{8,10},{9,11},{10,... | collective-permute-start | bytes 98312 | tf_op jit(solution)/shard_map/ppermute | solution.py:80
  104.4 5.0 %collective-permute-start.27 = (bf16[32,2048]{1,0:T(8,128)(2,1)S(1)}, bf16[32,2048]{1,0:T(8,128)(2,1)S(1)}, u32[]{:S(2)}, u32[]{:S(2)}) collective-permute-start(bf16[32,2048]{1,0:T(8,128)(2,1)S(1)} %maximum_select_fusion.14), channel_id=1, source_target_pairs={{0,8},{4,12},{8,0},{12,4},{16,24},{20,28},{24,16},{28,20},{1,9},{5... | collective-permute-start | bytes 393224 | tf_op jit(solution)/shard_map/ppermute | solution.py:80
  106.5 4.3 %collective-permute-start.6 = (bf16[16,2048]{1,0:T(8,128)(2,1)S(1)}, bf16[16,2048]{1,0:T(8,128)(2,1)S(1)}, u32[]{:S(2)}, u32[]{:S(2)}) collective-permute-start(bf16[16,2048]{1,0:T(8,128)(2,1)S(1)} %maximum_select_fusion.16), channel_id=1, source_target_pairs={{0,1},{1,0},{2,3},{3,2},{4,5},{5,4},{6,7},{7,6},{8,9},{9,8},{10,11... | collective-permute-start | bytes 196616 | tf_op jit(solution)/shard_map/ppermute | solution.py:80
  109.5 6.4 %collective-permute-start.28 = (bf16[64,2048]{1,0:T(8,128)(2,1)S(1)}, bf16[64,2048]{1,0:T(8,128)(2,1)S(1)}, u32[]{:S(2)}, u32[]{:S(2)}) collective-permute-start(bf16[64,2048]{1,0:T(8,128)(2,1)S(1)} %maximum_select_fusion.10), channel_id=1, source_target_pairs={{0,16},{4,20},{8,24},{12,28},{16,0},{20,4},{24,8},{28,12},{1,17},{... | collective-permute-start | bytes 786440 | tf_op jit(solution)/shard_map/ppermute | solution.py:80
  110.9 6.5 %collective-permute-start.7 = (bf16[32,2048]{1,0:T(8,128)(2,1)S(1)}, bf16[32,2048]{1,0:T(8,128)(2,1)S(1)}, u32[]{:S(2)}, u32[]{:S(2)}) collective-permute-start(bf16[32,2048]{1,0:T(8,128)(2,1)S(1)} %maximum_select_fusion.12), channel_id=1, source_target_pairs={{0,16},{4,20},{8,24},{12,28},{16,0},{20,4},{24,8},{28,12},{1,17},{... | collective-permute-start | bytes 393224 | tf_op jit(solution)/shard_map/ppermute | solution.py:80
  116.0 9.1 %collective-permute-start.29 = (bf16[128,2048]{1,0:T(8,128)(2,1)S(1)}, bf16[128,2048]{1,0:T(8,128)(2,1)S(1)}, u32[]{:S(2)}, u32[]{:S(2)}) collective-permute-start(bf16[128,2048]{1,0:T(8,128)(2,1)S(1)} %maximum_select_fusion.6), channel_id=1, source_target_pairs={{0,4},{4,0},{8,12},{12,8},{16,20},{20,16},{24,28},{28,24},{1,5},{5... | collective-permute-start | bytes 1572872 | tf_op jit(solution)/shard_map/ppermute | solution.py:80
  117.4 7.6 %collective-permute-start.8 = (bf16[64,2048]{1,0:T(8,128)(2,1)S(1)}, bf16[64,2048]{1,0:T(8,128)(2,1)S(1)}, u32[]{:S(2)}, u32[]{:S(2)}) collective-permute-start(bf16[64,2048]{1,0:T(8,128)(2,1)S(1)} %maximum_select_fusion.8), channel_id=1, source_target_pairs={{0,8},{4,12},{8,0},{12,4},{16,24},{20,28},{24,16},{28,20},{1,9},{5... | collective-permute-start | bytes 786440 | tf_op jit(solution)/shard_map/ppermute | solution.py:80
  125.1 32.2 %collective-permute-start.9 = (bf16[128,2048]{1,0:T(8,128)(2,1)S(1)}, bf16[128,2048]{1,0:T(8,128)(2,1)S(1)}, u32[]{:S(2)}, u32[]{:S(2)}) collective-permute-start(bf16[128,2048]{1,0:T(8,128)(2,1)S(1)} %maximum_select_fusion.4), channel_id=1, source_target_pairs={{0,4},{4,0},{8,12},{12,8},{16,20},{20,16},{24,28},{28,24},{1,5},{5... | collective-permute-start | bytes 1572872 | tf_op jit(solution)/shard_map/ppermute | solution.py:80
  155.6 2.0 copy-start.2
  156.8 31.3 %collective-permute-start.30 = (f32[128,2048]{1,0:T(8,128)}, f32[128,2048]{1,0:T(8,128)}, u32[]{:S(2)}, u32[]{:S(2)}) collective-permute-start(f32[128,2048]{1,0:T(8,128)} %constant_dynamic-slice_fusion), channel_id=1, source_target_pairs={{0,4},{4,0},{8,12},{12,8},{16,20},{20,16},{24,28},{28,24},{1,5},{5... | collective-permute-start | bytes 3145736 | tf_op jit(solution)/shard_map/ppermute | solution.py:80
  157.6 1.0 copy-start.5
  187.9 3.0 %collective-permute-start.10 = (f32[128,2048]{1,0:T(8,128)S(1)}, f32[128,2048]{1,0:T(8,128)S(1)}, u32[]{:S(2)}, u32[]{:S(2)}) collective-permute-start(f32[128,2048]{1,0:T(8,128)S(1)} %constant_dynamic-slice_fusion.4), channel_id=1, source_target_pairs={{0,4},{4,0},{8,12},{12,8},{16,20},{20,16},{24,28},{28,24},{1,5},{5... | collective-permute-start | bytes 3145736 | tf_op jit(solution)/shard_map/ppermute | solution.py:80
  189.8 8.6 %collective-permute-start.31 = (bf16[64,2048]{1,0:T(8,128)(2,1)S(1)}, bf16[64,2048]{1,0:T(8,128)(2,1)S(1)}, u32[]{:S(2)}, u32[]{:S(2)}) collective-permute-start(bf16[64,2048]{1,0:T(8,128)(2,1)S(1)} %dynamic-slice_convert_fusion), channel_id=1, source_target_pairs={{0,16},{4,20},{8,24},{12,28},{16,0},{20,4},{24,8},{28,12},{1,17},{... | collective-permute-start | bytes 786440 | tf_op jit(solution)/shard_map/ppermute | solution.py:80
  191.1 9.1 %collective-permute-start.11 = (bf16[64,2048]{1,0:T(8,128)(2,1)S(1)}, bf16[64,2048]{1,0:T(8,128)(2,1)S(1)}, u32[]{:S(2)}, u32[]{:S(2)}) collective-permute-start(bf16[64,2048]{1,0:T(8,128)(2,1)S(1)} %dynamic-slice_convert_fusion.2), channel_id=1, source_target_pairs={{0,8},{4,12},{8,0},{12,4},{16,24},{20,28},{24,16},{28,20},{1,9},{5... | collective-permute-start | bytes 786440 | tf_op jit(solution)/shard_map/ppermute | solution.py:80
  198.6 5.0 %collective-permute-start.32 = (bf16[32,2048]{1,0:T(8,128)(2,1)S(1)}, bf16[32,2048]{1,0:T(8,128)(2,1)S(1)}, u32[]{:S(2)}, u32[]{:S(2)}) collective-permute-start(bf16[32,2048]{1,0:T(8,128)(2,1)S(1)} %dynamic-slice_convert_fusion.4), channel_id=1, source_target_pairs={{0,8},{4,12},{8,0},{12,4},{16,24},{20,28},{24,16},{28,20},{1,9},{5... | collective-permute-start | bytes 393224 | tf_op jit(solution)/shard_map/ppermute | solution.py:80
  200.2 5.1 %collective-permute-start.12 = (bf16[32,2048]{1,0:T(8,128)(2,1)S(1)}, bf16[32,2048]{1,0:T(8,128)(2,1)S(1)}, u32[]{:S(2)}, u32[]{:S(2)}) collective-permute-start(bf16[32,2048]{1,0:T(8,128)(2,1)S(1)} %dynamic-slice_convert_fusion.6), channel_id=1, source_target_pairs={{0,16},{4,20},{8,24},{12,28},{16,0},{20,4},{24,8},{28,12},{1,17},{... | collective-permute-start | bytes 393224 | tf_op jit(solution)/shard_map/ppermute | solution.py:80
  203.6 36.7 %copy-start.4 = (bf16[256,2048]{1,0:T(8,128)(2,1)S(1)}, bf16[256,2048]{1,0:T(8,128)(2,1)}, u32[]{:S(2)}) copy-start(bf16[256,2048]{1,0:T(8,128)(2,1)} %copy-done.3) | copy-start | bytes 3145732
  203.6 36.7 %copy-start.6 = (bf16[256,2048]{1,0:T(8,128)(2,1)S(1)}, bf16[256,2048]{1,0:T(8,128)(2,1)}, u32[]{:S(2)}) copy-start(bf16[256,2048]{1,0:T(8,128)(2,1)} %copy-done.5) | copy-start | bytes 3145732
  203.6 36.7 %copy-start.8 = (bf16[256,6144]{1,0:T(8,128)(2,1)S(1)}, bf16[256,6144]{1,0:T(8,128)(2,1)}, u32[]{:S(2)}) copy-start(bf16[256,6144]{1,0:T(8,128)(2,1)} %fusion.1) | copy-start | bytes 9437188
  203.7 4.3 %collective-permute-start.33 = (bf16[16,2048]{1,0:T(8,128)(2,1)S(1)}, bf16[16,2048]{1,0:T(8,128)(2,1)S(1)}, u32[]{:S(2)}, u32[]{:S(2)}) collective-permute-start(bf16[16,2048]{1,0:T(8,128)(2,1)S(1)} %dynamic-slice_convert_fusion.8), channel_id=1, source_target_pairs={{0,1},{1,0},{2,3},{3,2},{4,5},{5,4},{6,7},{7,6},{8,9},{9,8},{10,11... | collective-permute-start | bytes 196616 | tf_op jit(solution)/shard_map/ppermute | solution.py:80
  205.4 5.5 %collective-permute-start.13 = (bf16[16,2048]{1,0:T(8,128)(2,1)S(1)}, bf16[16,2048]{1,0:T(8,128)(2,1)S(1)}, u32[]{:S(2)}, u32[]{:S(2)}) collective-permute-start(bf16[16,2048]{1,0:T(8,128)(2,1)S(1)} %dynamic-slice_convert_fusion.9), channel_id=1, source_target_pairs={{0,1},{1,0},{2,3},{3,2},{4,5},{5,4},{6,7},{7,6},{8,9},{9,8},{10,11... | collective-permute-start | bytes 196616 | tf_op jit(solution)/shard_map/ppermute | solution.py:80
  208.1 4.9 %collective-permute-start.34 = (bf16[8,2048]{1,0:T(8,128)(2,1)S(1)}, bf16[8,2048]{1,0:T(8,128)(2,1)S(1)}, u32[]{:S(2)}, u32[]{:S(2)}) collective-permute-start(bf16[8,2048]{1,0:T(8,128)(2,1)S(1)} %dynamic-slice_convert_fusion.10), channel_id=1, source_target_pairs={{0,2},{1,3},{2,0},{3,1},{4,6},{5,7},{6,4},{7,5},{8,10},{9,11},{10,... | collective-permute-start | bytes 98312 | tf_op jit(solution)/shard_map/ppermute | solution.py:80
  210.9 5.1 %collective-permute-start.14 = (bf16[8,2048]{1,0:T(8,128)(2,1)S(1)}, bf16[8,2048]{1,0:T(8,128)(2,1)S(1)}, u32[]{:S(2)}, u32[]{:S(2)}) collective-permute-start(bf16[8,2048]{1,0:T(8,128)(2,1)S(1)} %dynamic-slice_convert_fusion.11), channel_id=1, source_target_pairs={{0,2},{1,3},{2,0},{3,1},{4,6},{5,7},{6,4},{7,5},{8,10},{9,11},{10,... | collective-permute-start | bytes 98312 | tf_op jit(solution)/shard_map/ppermute | solution.py:80
  216.1 5.0 %collective-permute-start.15 = (bf16[8,2048]{1,0:T(8,128)(2,1)S(1)}, bf16[8,2048]{1,0:T(8,128)(2,1)S(1)}, u32[]{:S(2)}, u32[]{:S(2)}) collective-permute-start(bf16[8,2048]{1,0:T(8,128)(2,1)S(1)} %get-tuple-element.2), channel_id=1, source_target_pairs={{0,2},{1,3},{2,0},{3,1},{4,6},{5,7},{6,4},{7,5},{8,10},{9,11},{10,... | collective-permute-start | bytes 98312 | tf_op jit(solution)/shard_map/ppermute | solution.py:80
  217.7 4.8 %collective-permute-start.35 = (bf16[8,2048]{1,0:T(8,128)(2,1)S(1)}, bf16[8,2048]{1,0:T(8,128)(2,1)S(1)}, u32[]{:S(2)}, u32[]{:S(2)}) collective-permute-start(bf16[8,2048]{1,0:T(8,128)(2,1)S(1)} %get-tuple-element.3), channel_id=1, source_target_pairs={{0,2},{1,3},{2,0},{3,1},{4,6},{5,7},{6,4},{7,5},{8,10},{9,11},{10,... | collective-permute-start | bytes 98312 | tf_op jit(solution)/shard_map/ppermute | solution.py:80
  221.1 4.3 %collective-permute-start.16 = (bf16[16,2048]{1,0:T(8,128)(2,1)S(1)}, bf16[16,2048]{1,0:T(8,128)(2,1)S(1)}, u32[]{:S(2)}, u32[]{:S(2)}) collective-permute-start(bf16[16,2048]{1,0:T(8,128)(2,1)S(1)} %maximum_select_fusion.17), channel_id=1, source_target_pairs={{0,1},{1,0},{2,3},{3,2},{4,5},{5,4},{6,7},{7,6},{8,9},{9,8},{10,11... | collective-permute-start | bytes 196616 | tf_op jit(solution)/shard_map/ppermute | solution.py:80
  222.5 5.1 %collective-permute-start.36 = (bf16[16,2048]{1,0:T(8,128)(2,1)S(1)}, bf16[16,2048]{1,0:T(8,128)(2,1)S(1)}, u32[]{:S(2)}, u32[]{:S(2)}) collective-permute-start(bf16[16,2048]{1,0:T(8,128)(2,1)S(1)} %maximum_select_fusion.19), channel_id=1, source_target_pairs={{0,1},{1,0},{2,3},{3,2},{4,5},{5,4},{6,7},{7,6},{8,9},{9,8},{10,11... | collective-permute-start | bytes 196616 | tf_op jit(solution)/shard_map/ppermute | solution.py:80
  225.4 6.4 %collective-permute-start.17 = (bf16[32,2048]{1,0:T(8,128)(2,1)S(1)}, bf16[32,2048]{1,0:T(8,128)(2,1)S(1)}, u32[]{:S(2)}, u32[]{:S(2)}) collective-permute-start(bf16[32,2048]{1,0:T(8,128)(2,1)S(1)} %maximum_select_fusion.13), channel_id=1, source_target_pairs={{0,16},{4,20},{8,24},{12,28},{16,0},{20,4},{24,8},{28,12},{1,17},{... | collective-permute-start | bytes 393224 | tf_op jit(solution)/shard_map/ppermute | solution.py:80
  227.6 6.1 %collective-permute-start.37 = (bf16[32,2048]{1,0:T(8,128)(2,1)S(1)}, bf16[32,2048]{1,0:T(8,128)(2,1)S(1)}, u32[]{:S(2)}, u32[]{:S(2)}) collective-permute-start(bf16[32,2048]{1,0:T(8,128)(2,1)S(1)} %maximum_select_fusion.15), channel_id=1, source_target_pairs={{0,8},{4,12},{8,0},{12,4},{16,24},{20,28},{24,16},{28,20},{1,9},{5... | collective-permute-start | bytes 393224 | tf_op jit(solution)/shard_map/ppermute | solution.py:80
  231.9 6.4 %collective-permute-start.18 = (bf16[64,2048]{1,0:T(8,128)(2,1)S(1)}, bf16[64,2048]{1,0:T(8,128)(2,1)S(1)}, u32[]{:S(2)}, u32[]{:S(2)}) collective-permute-start(bf16[64,2048]{1,0:T(8,128)(2,1)S(1)} %maximum_select_fusion.9), channel_id=1, source_target_pairs={{0,8},{4,12},{8,0},{12,4},{16,24},{20,28},{24,16},{28,20},{1,9},{5... | collective-permute-start | bytes 786440 | tf_op jit(solution)/shard_map/ppermute | solution.py:80
  233.7 6.4 %collective-permute-start.38 = (bf16[64,2048]{1,0:T(8,128)(2,1)S(1)}, bf16[64,2048]{1,0:T(8,128)(2,1)S(1)}, u32[]{:S(2)}, u32[]{:S(2)}) collective-permute-start(bf16[64,2048]{1,0:T(8,128)(2,1)S(1)} %maximum_select_fusion.11), channel_id=1, source_target_pairs={{0,16},{4,20},{8,24},{12,28},{16,0},{20,4},{24,8},{28,12},{1,17},{... | collective-permute-start | bytes 786440 | tf_op jit(solution)/shard_map/ppermute | solution.py:80
  238.5 21.0 %collective-permute-start.19 = (bf16[128,2048]{1,0:T(8,128)(2,1)S(1)}, bf16[128,2048]{1,0:T(8,128)(2,1)S(1)}, u32[]{:S(2)}, u32[]{:S(2)}) collective-permute-start(bf16[128,2048]{1,0:T(8,128)(2,1)S(1)} %maximum_select_fusion.5), channel_id=1, source_target_pairs={{0,4},{4,0},{8,12},{12,8},{16,20},{20,16},{24,28},{28,24},{1,5},{5... | collective-permute-start | bytes 1572872 | tf_op jit(solution)/shard_map/ppermute | solution.py:80
  240.3 19.5 %collective-permute-start.39 = (bf16[128,2048]{1,0:T(8,128)(2,1)S(1)}, bf16[128,2048]{1,0:T(8,128)(2,1)S(1)}, u32[]{:S(2)}, u32[]{:S(2)}) collective-permute-start(bf16[128,2048]{1,0:T(8,128)(2,1)S(1)} %maximum_select_fusion.7), channel_id=1, source_target_pairs={{0,4},{4,0},{8,12},{12,8},{16,20},{20,16},{24,28},{28,24},{1,5},{5... | collective-permute-start | bytes 1572872 | tf_op jit(solution)/shard_map/ppermute | solution.py:80
  (1 other events, 1.0 us)
